TPU v7x, 256 devices: a whole 4x4x8 slice. The times are simulated.
256 devices in a mesh: row: 16 (over x_lo, y, core), col: 16 (over z, x_hi).
Axes of the slice: x: 4 (x_hi: 2, x_lo: 2; x = x_hi * 2 + x_lo), y: 4, z: 8, core: 2. Of those that a mesh axis runs over, the one named last changes fastest.
Arguments:
- node_feats: bfloat16 [65536, 512], P(('row', 'col')), may hold values from -6 to 6
- cotangent: bfloat16 [65536, 512], P(('row', 'col')), may hold values from -6 to 6
- edge_base: bfloat16 [512, 512], replicated, may hold values from -0.25 to 0.25
- edge_down: bfloat16 [512, 16], replicated, may hold values from -0.25 to 0.25
- edge_up: bfloat16 [16, 512], replicated, may hold values from -1.5 to 1.5
- node_base: bfloat16 [1024, 512], replicated, may hold values from -0.1875 to 0.1875
- node_down: bfloat16 [1024, 16], replicated, may hold values from -0.1875 to 0.1875
- node_up: bfloat16 [16, 512], replicated, may hold values from -1.5 to 1.5
- tile_weight: bfloat16 [16, 16, 64, 128, 128], P('row', 'col'), may hold values from 0 to 1, as said below
- tile_place: int32 [16, 16, 64, 2], P('row', 'col'), may hold values from 0 to 31, as said below
- tile_count: int32 [16, 16], P('row', 'col'), may hold values from 1 to 64, as said below
Outputs:
- new_feats: bfloat16 [65536, 512], P(('row', 'col'))
- feat_grad: bfloat16 [65536, 512], P(('row', 'col'))
- edge_down_grad: float32 [512, 16], replicated
- edge_up_grad: float32 [16, 512], replicated
- node_down_grad: float32 [1024, 16], replicated
- node_up_grad: float32 [16, 512], replicated
Inputs may be any that keep to these rules, and one draw needn't show every extreme that they name: `tile_place`: on each device the slots below its tile_count name distinct tiles; entry 0 is a tile row below 32, entry 1 a tile column below 32. `tile_count`: some device has all 64 slots live in every draw. `tile_weight`: Nonnegative; slots at or beyond a device's tile_count hold values that are no part of the graph.
All inputs are finite; a program needn't handle non-finite values.
Results may differ from a plain program's by a relative error of at most 0.035.
Values may be sent and summed in bfloat16 or wider, within the bound.
No kernel may reach another device: no remote copies, remote signals or barrier semaphores. Data moves between devices by JAX's collectives and lax.ppermute only.
A program may use at most 128 MiB of HBM per device.

v0:
```python
import math

import jax
import jax.numpy as jnp
from jax import lax
from jax.sharding import PartitionSpec as P


def silu_slope(values):
    sigma = jax.nn.sigmoid(values)
    return sigma * (1.0 + values * (1.0 - sigma))


def across(left, right):
    return lax.dot_general(
        left, right, (((0,), (0,)), ((), ())), preferred_element_type=jnp.float32
    )


def times_transposed(left, right):
    return lax.dot_general(
        left, right, (((1,), (1,)), ((), ())), preferred_element_type=jnp.float32
    )


def prepare(tile_stack, keys, others, alive_mask, limit_value):
    sort_keys = jnp.where(alive_mask, keys, limit_value)
    sort_order = jnp.argsort(sort_keys, stable=True)
    return (
        tile_stack[sort_order],
        sort_keys[sort_order],
        others[sort_order],
        alive_mask[sort_order],
    )


def fold_range(running, pieces, arranged, low_tile, span, transpose):
    ordered, keys, others, alive_mask = arranged
    slot_count = ordered.shape[0]
    group_size = math.gcd(slot_count, 16)
    inside = alive_mask & (keys >= low_tile) & (keys < low_tile + span)
    lower_end = jnp.sum((alive_mask & (keys < low_tile)).astype(jnp.int32))
    upper_end = lower_end + jnp.sum(inside.astype(jnp.int32))

    def one_group(group_index, carried):
        begin_slot = group_index * group_size
        weights_group = lax.dynamic_slice_in_dim(ordered, begin_slot, group_size, 0)
        keep_mask = lax.dynamic_slice_in_dim(inside, begin_slot, group_size, 0)
        key_part = lax.dynamic_slice_in_dim(keys, begin_slot, group_size, 0)
        other_part = lax.dynamic_slice_in_dim(others, begin_slot, group_size, 0)
        weights_group = jnp.where(
            keep_mask[:, None, None], weights_group, jnp.zeros_like(weights_group)
        )
        fetch_index = key_part - low_tile
        fetched = pieces[jnp.clip(fetch_index, 0, pieces.shape[0] - 1)]
        if transpose:
            products = jnp.einsum(
                "gij,gid->gjd", weights_group, fetched, preferred_element_type=jnp.float32
            )
        else:
            products = jnp.einsum(
                "gij,gjd->gid", weights_group, fetched, preferred_element_type=jnp.float32
            )
        return carried.at[jnp.clip(other_part, 0, carried.shape[0] - 1)].add(products)

    return lax.fori_loop(
        lower_end // group_size, (upper_end + group_size - 1) // group_size, one_group, running
    )


def body(
    node_feats,
    cotangent,
    edge_base,
    edge_down,
    edge_up,
    node_base,
    node_down,
    node_up,
    tile_weight,
    tile_place,
    tile_count,
):
    node_rows, feature_width = node_feats.shape
    tile_stack = tile_weight[0, 0]
    places = tile_place[0, 0]
    tile_total = tile_count[0, 0]
    slot_count, tile_size = (tile_stack.shape[0], tile_stack.shape[1])
    alive_mask = jnp.arange(slot_count, dtype=jnp.int32) < tile_total
    row_tiles = lax.axis_size("col") * node_rows // tile_size
    col_tiles = lax.axis_size("row") * node_rows // tile_size
    low_edge = jnp.dot(node_feats, edge_down, preferred_element_type=jnp.float32).astype(
        jnp.bfloat16
    )
    edge_pre = jnp.dot(node_feats, edge_base, preferred_element_type=jnp.float32) + jnp.dot(
        low_edge, edge_up, preferred_element_type=jnp.float32
    )
    message = jax.nn.silu(edge_pre).astype(jnp.bfloat16)
    empty_rows = jnp.zeros((row_tiles, tile_size, feature_width), jnp.float32)
    column_block = lax.all_gather(message, "row", axis=0, tiled=True).reshape(
        col_tiles, tile_size, feature_width
    )
    forward_order = prepare(tile_stack, places[:, 1], places[:, 0], alive_mask, col_tiles)
    partial_value = fold_range(empty_rows, column_block, forward_order, 0, col_tiles, False)
    summed = lax.psum_scatter(
        partial_value.reshape(row_tiles * tile_size, feature_width).astype(jnp.bfloat16),
        "col",
        scatter_dimension=0,
        tiled=True,
    )
    joined = jnp.concatenate([node_feats, summed], axis=1)
    low_node = jnp.dot(joined, node_down, preferred_element_type=jnp.float32).astype(jnp.bfloat16)
    node_pre = jnp.dot(joined, node_base, preferred_element_type=jnp.float32) + jnp.dot(
        low_node, node_up, preferred_element_type=jnp.float32
    )
    new_feats = (node_feats.astype(jnp.float32) + jax.nn.silu(node_pre)).astype(jnp.bfloat16)
    node_slope = (cotangent.astype(jnp.float32) * silu_slope(node_pre)).astype(jnp.bfloat16)
    node_mix = times_transposed(node_slope, node_up).astype(jnp.bfloat16)
    joined_grad = times_transposed(node_slope, node_base) + times_transposed(node_mix, node_down)
    agg_grad = joined_grad[:, feature_width:].astype(jnp.bfloat16)
    factor = 1.0 / math.sqrt(node_rows * lax.axis_size("row") * lax.axis_size("col"))
    empty_cols = jnp.zeros((col_tiles, tile_size, feature_width), jnp.float32)
    row_block = lax.all_gather(agg_grad, "col", axis=0, tiled=True).reshape(
        row_tiles, tile_size, feature_width
    )
    backward_order = prepare(tile_stack, places[:, 0], places[:, 1], alive_mask, row_tiles)
    reverse_part = fold_range(empty_cols, row_block, backward_order, 0, row_tiles, True)
    message_grad = lax.psum_scatter(
        reverse_part.reshape(col_tiles * tile_size, feature_width).astype(jnp.bfloat16),
        "row",
        scatter_dimension=0,
        tiled=True,
    ).astype(jnp.float32)
    edge_slope = (message_grad * silu_slope(edge_pre)).astype(jnp.bfloat16)
    edge_mix = times_transposed(edge_slope, edge_up).astype(jnp.bfloat16)
    adapter_sums = lax.psum(
        (
            across(node_feats, edge_mix),
            across(low_edge, edge_slope),
            across(joined, node_mix),
            across(low_node, node_slope),
        ),
        ("row", "col"),
    )
    feat_grad = (
        cotangent.astype(jnp.float32)
        + joined_grad[:, :feature_width]
        + times_transposed(edge_slope, edge_base)
        + times_transposed(edge_mix, edge_down)
    ).astype(jnp.bfloat16)
    return (
        new_feats,
        feat_grad,
        adapter_sums[0] * factor,
        adapter_sums[1] * factor,
        adapter_sums[2] * factor,
        adapter_sums[3] * factor,
    )


def solution(mesh):
    placed = (
        P(("row", "col"), None),
        P(("row", "col"), None),
        P(),
        P(),
        P(),
        P(),
        P(),
        P(),
        P("row", "col", None, None, None),
        P("row", "col", None, None),
        P("row", "col"),
    )
    return jax.shard_map(
        body,
        mesh=mesh,
        in_specs=placed,
        out_specs=(P(("row", "col"), None), P(("row", "col"), None), P(), P(), P(), P()),
        check_vma=False,
    )
```

profile of v0, /device:TPU:1, one launch (start us, length us, event | category | flops | bytes accessed | tf_op | source)
XLA Modules:
  0.0 1024.2 jit_solution(15889899230155985471)
XLA Ops:
  23.7 32.4 %all-gather.3.cloned.1.call-done = bf16[4096,512]{1,0:T(8,128)(2,1)} async-done(((bf16[256,512]{1,0:T(8,128)(2,1)}), bf16[4096,512]{1,0:T(8,128)(2,1)}) %all-gather.3.cloned.1.call-update) | async-done | bytes 4194320 | tf_op jit(solution)/shard_map/all_gather | solution.py:100
  56.1 4.3 broadcast.39.clone
  60.4 54.5 %while.20 = (s32[]{:T(128)}, f32[32,128,512]{2,1,0:T(8,128)}, s32[]{:T(128)}, s32[64]{0:T(128)S(1)}, pred[64]{0:T(512)(128)(4,1)S(1)}, /*index=5*/bf16[64,128,12...) while((s32[]{:T(128)}, f32[32,128,512]{2,1,0:T(8,128)}, ...), condition=%wide.region_5.6_spmd, body=%wide.region_3.5_spmd.sunk | while | flops 269747328 | bytes 23597736 | solution.py:66
  64.7 4.5 fusion.64
  69.2 9.3 scatter_fusion
  82.9 4.5 fusion.64
  87.3 9.5 scatter_fusion
  101.1 4.5 fusion.64
  105.6 9.3 scatter_fusion
  114.9 6.0 convert_element_type.67
  121.9 225.2 %reduce-scatter.3.cloned.1.call-done = bf16[256,512]{1,0:T(8,128)(2,1)} async-done(((bf16[4096,512]{1,0:T(8,128)(2,1)}), bf16[256,512]{1,0:T(8,128)(2,1)}) %reduce-scatter.3.cloned.1.call-update) | async-done | bytes 262160 | tf_op jit(solution)/shard_map/reduce_scatter | solution.py:105
  366.1 87.5 %all-gather.5.cloned.1.call-done = bf16[4096,512]{1,0:T(8,128)(2,1)} async-done(((bf16[256,512]{1,0:T(8,128)(2,1)}), bf16[4096,512]{1,0:T(8,128)(2,1)}) %all-gather.5.cloned.1.call-update) | async-done | bytes 4194320 | tf_op jit(solution)/shard_map/all_gather | solution.py:123
  453.6 4.3 broadcast.39
  457.8 57.9 %while.21 = (s32[]{:T(128)}, f32[32,128,512]{2,1,0:T(8,128)}, s32[]{:T(128)}, s32[64]{0:T(128)S(1)}, pred[64]{0:T(512)(128)(4,1)S(1)}, /*index=5*/bf16[64,128,12...) while((s32[]{:T(128)}, f32[32,128,512]{2,1,0:T(8,128)}, ...), condition=%wide.region_12.13_spmd, body=%wide.region_10.12_spmd.sunk | while | flops 269747328 | bytes 25694888 | solution.py:66
  463.5 4.3 fusion.67
  467.8 9.4 scatter_fusion.1
  483.0 4.3 fusion.67
  487.3 9.3 scatter_fusion.1
  502.3 4.3 fusion.67
  506.6 9.2 scatter_fusion.1
  515.8 6.0 convert_element_type.76
  523.6 174.8 %all-reduce.4.cloned.1.call-done = f32[1024,16]{0,1:T(8,128)} async-done(((f32[1024,16]{0,1:T(8,128)}), f32[1024,16]{0,1:T(8,128)}) %all-reduce.4.cloned.1.call-update) | async-done | bytes 65552 | tf_op jit(solution)/shard_map/psum | solution.py:136
  699.9 63.0 %reduce-scatter.5.cloned.1.call-done = bf16[256,512]{1,0:T(8,128)(2,1)} async-done(((bf16[4096,512]{1,0:T(8,128)(2,1)}), bf16[256,512]{1,0:T(8,128)(2,1)}) %reduce-scatter.5.cloned.1.call-update) | async-done | bytes 262160 | tf_op jit(solution)/shard_map/reduce_scatter | solution.py:128
  770.2 244.4 %all-reduce.6.cloned.1.call-done = (f32[512,16]{0,1:T(8,128)}, f32[16,512]{1,0:T(8,128)}, f32[16,512]{1,0:T(8,128)}) async-done(((f32[512,16]{0,1:T(8,128)}, f32[16,512]{1,0:T(8,128)}, f32[16,512]{1,0:T(8,128)}), (f32[512,16]{0,1:T(8,128)}, f32[16,512]{1,0:T(8,128)}, f32[16,512]{1,0:T(8,128)})) %all-reduce.6.cloned.1.call-update) | async-done | bytes 98320 | tf_op jit(solution)/shard_map/psum | solution.py:136
  (108 shorter events, 71.3 us)
Async XLA Ops:
  7.2 14.3 %copy-start = (bf16[1,1,64,128,128]{4,3,2,1,0:T(8,128)(2,1)S(1)}, bf16[1,1,64,128,128]{4,3,2,1,0:T(8,128)(2,1)}, u32[]{:S(2)}) copy-start(bf16[1,1,64,128,128]{4,3,2,1,0:T(8,128)(2,1)} %param.23) | copy-start | bytes 6291460
  7.2 5.3 copy-start.10
  7.2 48.9 %all-gather.3.cloned.1.call-start = ((), (), s32[]{:S(2)}) async-start(), calls=%async_computation.2 | async-start | bytes 4456448 | tf_op jit(solution)/shard_map/all_gather | solution.py:100
  11.8 335.3 %reduce-scatter.3.cloned.1.call-start = ((), (), s32[]{:S(2)}) async-start(), calls=%async_computation.3 | async-start | bytes 4456448 | tf_op jit(solution)/shard_map/reduce_scatter | solution.py:105
  120.9 0.9 copy-start.1
  120.9 227.3 %copy-start.6 = (bf16[1024,16]{0,1:T(8,128)(2,1)S(1)}, bf16[1024,16]{0,1:T(8,128)(2,1)}, u32[]{:S(2)}) copy-start(bf16[1024,16]{0,1:T(8,128)(2,1)} %param.21) | copy-start | bytes 98308
  120.9 227.5 %copy-start.7 = (bf16[16,512]{1,0:T(8,128)(2,1)S(1)}, bf16[16,512]{1,0:T(8,128)(2,1)}, u32[]{:S(2)}) copy-start(bf16[16,512]{1,0:T(8,128)(2,1)} %param.22) | copy-start | bytes 49156
  120.9 332.6 %all-gather.5.cloned.1.call-start = ((), (), s32[]{:S(2)}) async-start(), calls=%async_computation.4 | async-start | bytes 4456448 | tf_op jit(solution)/shard_map/all_gather | solution.py:123
  347.1 4.2 copy-start.5
  351.3 13.1 %copy-start.4 = (bf16[256,512]{1,0:T(8,128)(2,1)}, bf16[256,512]{1,0:T(8,128)(2,1)S(1)}, u32[]{:S(2)}) copy-start(bf16[256,512]{1,0:T(8,128)(2,1)S(1)} %get-tuple-element.149) | copy-start | bytes 786436
  352.3 1.0 copy-start.2
  354.1 344.4 %all-reduce.4.cloned.1.call-start = ((), (), s32[]{:S(2)}) async-start(), calls=%async_computation.6 | async-start | bytes 131072 | tf_op jit(solution)/shard_map/psum | solution.py:136
  366.0 396.8 %reduce-scatter.5.cloned.1.call-start = ((), (), s32[]{:S(2)}) async-start(), calls=%async_computation.5 | async-start | bytes 4456448 | tf_op jit(solution)/shard_map/reduce_scatter | solution.py:128
  521.8 242.5 %copy-start.3 = (f32[256,1024]{1,0:T(8,128)S(1)}, f32[256,1024]{1,0:T(8,128)}, u32[]{:S(2)}) copy-start(f32[256,1024]{1,0:T(8,128)} %copy-done.2) | copy-start | bytes 3145732
  521.8 244.7 %copy-start.9 = (bf16[16,512]{1,0:T(8,128)(2,1)S(1)}, bf16[16,512]{1,0:T(8,128)(2,1)}, u32[]{:S(2)}) copy-start(bf16[16,512]{1,0:T(8,128)(2,1)} %param.19) | copy-start | bytes 49156
  521.8 246.4 %copy-start.8 = (bf16[512,16]{0,1:T(8,128)(2,1)S(1)}, bf16[512,16]{0,1:T(8,128)(2,1)}, u32[]{:S(2)}) copy-start(bf16[512,16]{0,1:T(8,128)(2,1)} %param.18) | copy-start | bytes 49156
  521.8 492.8 %all-reduce.6.cloned.1.call-start = ((), (), s32[]{:S(2)}) async-start(), calls=%async_computation.7 | async-start | bytes 196608 | tf_op jit(solution)/shard_map/psum | solution.py:136
Sparse Core Ops, SparseCore 0:
  11.9 44.1 all-gather.2
  121.0 226.0 reduce-scatter.2
  354.2 99.3 all-gather.4
  460.4 238.0 all-reduce.3
  701.0 61.8 reduce-scatter.4
  770.4 244.1 all-reduce.5
where the time goes:
time: 1030 us; the launch traced here: 1020 us
  waiting for transfers between devices  827 us (80%)
  other arithmetic  79.4 us (8%)
  local copies, waits for them, and re-layouts  50.8 us (5%)
  matrix products  43.5 us (4%)
  between operations  22.7 us (2%)
    psum x2, waiting for transfers between devices, body(): lax.psum((across(node_feats, edge_mix), across(low_edge, edge_slope), acr...  419 us
    reduce_scatter x1, waiting for transfers between devices, body(): lax.psum_scatter(partial_value.reshape(row_tiles * tile_size, feature_wid...  225 us
    all_gather x1, waiting for transfers between devices, body(): lax.all_gather(agg_grad, 'col', axis=0, tiled=True)  87.5 us
    reduce_scatter x1, waiting for transfers between devices, body(): lax.psum_scatter(reverse_part.reshape(col_tiles * tile_size, feature_widt...  63 us
    scatter-add x6, other arithmetic, one_group(): carried.at[jnp.clip(other_part, 0, carried.shape[0] - 1)].add(products)  56 us
    all_gather x1, waiting for transfers between devices, body(): lax.all_gather(message, 'row', axis=0, tiled=True)  32.4 us
    gather x6, local copies, waits for them, and re-layouts, one_group(): fetched = pieces[jnp.clip(fetch_index, 0, pieces.shape[0] - 1)]  25 us
  transfers between devices with their start and end apart: 6, of which 6 were waited for; matrix products, arithmetic and copies ran while one was open for 9% of the time, Pallas kernels for 0%

commit v1 on v0

v1 whole, which is shorter than its diff:
```python
import math

import jax
import jax.numpy as jnp
from jax import lax
from jax.experimental import pallas as pl
from jax.experimental.pallas import tpu as pltpu
from jax.sharding import Mesh, PartitionSpec as P

BF, F32 = jnp.bfloat16, jnp.float32
UNROLL = 8
MIB = 1 << 20
ALL = ("xly", "co", "zh", "zl", "xh")
ROW, COL = ("xly", "co"), ("zh", "zl", "xh")
ROW_GROUP = ("xly", "co", "zl")
COL_GROUP = ("co", "zh", "zl", "xh")


def dot(left, right):
    return jnp.dot(left, right, preferred_element_type=F32)


def across(left, right):
    return lax.dot_general(left, right, (((0,), (0,)), ((), ())), preferred_element_type=F32)


def times_transposed(left, right):
    return lax.dot_general(left, right, (((1,), (1,)), ((), ())), preferred_element_type=F32)


def sigmoid(values):
    return 1.0 / (1.0 + jnp.exp(-values))


def silu_slope(values):
    sigma = sigmoid(values)
    return sigma * (1.0 + values * (1.0 - sigma))


def call(kernel, out_shape, *args, scratch=(), smem=0, vmem=40, flops=0, name=None):
    moved = sum(a.size * a.dtype.itemsize for a in args)
    moved += sum(math.prod(s.shape) * s.dtype.itemsize for s in jax.tree.leaves(out_shape))
    return pl.pallas_call(
        kernel,
        out_shape=out_shape,
        in_specs=[pl.BlockSpec(memory_space=pltpu.SMEM)] * smem
        + [pl.BlockSpec(memory_space=pltpu.VMEM)] * (len(args) - smem),
        out_specs=jax.tree.map(lambda _: pl.BlockSpec(memory_space=pltpu.VMEM), out_shape),
        scratch_shapes=list(scratch),
        compiler_params=pltpu.CompilerParams(vmem_limit_bytes=vmem * MIB),
        cost_estimate=pl.CostEstimate(flops=flops, bytes_accessed=moved, transcendentals=0),
        name=name,
    )(*args)


def message_kernel(feats, base, down, up, pieces, pre_out, low_out):
    low = dot(feats[...], down[...]).astype(BF)
    pre = dot(feats[...], base[...]) + dot(low, up[...])
    message = (pre * sigmoid(pre)).astype(BF)
    low_out[...] = low
    pre_out[...] = pre
    quarters, width = 4, pieces.shape[-1]
    for i in range(pieces.shape[0]):
        q = i % quarters
        pieces[i] = message[:, q * width : (q + 1) * width]


def tile_kernel(backward, here, meta, w0, w1, w2, w3, source, out, total):
    co, zl = here[0], here[1]
    rows = out.shape[0]
    block_rows = rows // 2
    chunk = 512
    slots = w0.shape[0]

    def clear(i, carry):
        total[pl.ds(pl.multiple_of(i * chunk, chunk), chunk), :] = jnp.zeros(
            (chunk, total.shape[1]), F32
        )
        return carry

    lax.fori_loop(0, rows // chunk, clear, 0)

    for weights, other_co, other_zl in ((w0, 0, 0), (w1, 1, 0), (w2, 0, 1), (w3, 1, 1)):
        owner_co = co ^ other_co
        owner_zl = zl ^ other_zl
        owner = owner_co * 2 + owner_zl
        count = meta[owner, 2 * slots]

        def group(i, carry, weights=weights, owner=owner, owner_co=owner_co, owner_zl=owner_zl, count=count):
            products, places = [], []
            for j in range(UNROLL):
                slot = i * UNROLL + j
                live = slot < count
                tile_row = jnp.where(live, meta[owner, 2 * slot], 0)
                tile_col = jnp.where(live, meta[owner, 2 * slot + 1], 0)
                row_at = owner_co * block_rows + tile_row * 128
                col_at = (tile_col >> 1) * 512 + owner_zl * 256 + (tile_col & 1) * 128
                from_at, to_at = (row_at, col_at) if backward else (col_at, row_at)
                places.append(pl.multiple_of(jnp.where(live, to_at, rows), 128))
                block = source[pl.ds(pl.multiple_of(from_at, 128), 128), :]
                tile = weights[slot]
                products.append(across(tile, block) if backward else dot(tile, block))
            for product, at in zip(products, places):
                total[pl.ds(at, 128), :] += product
            return carry

        lax.fori_loop(0, (count + UNROLL - 1) // UNROLL, group, 0)

    def finish(i, carry):
        at = pl.ds(pl.multiple_of(i * chunk, chunk), chunk)
        out[at, :] = total[at, :].astype(BF)
        return carry

    lax.fori_loop(0, rows // chunk, finish, 0)


def node_kernel(feats, cot, parts, base, down, up, new_out, pieces, partial_out, grads):
    n_col = parts.shape[0] // 2
    width = parts.shape[-1]
    quarters = []
    for s_co in range(2):
        for s_zl in range(2):
            value = None
            for zh in range(n_col // 4):
                for xh in range(2):
                    term = parts[s_co * n_col + zh * 4 + s_zl * 2 + xh].astype(F32)
                    value = term if value is None else value + term
            quarters.append(value.astype(BF))
    joined = jnp.concatenate([feats[...]] + quarters, axis=1)
    low = dot(joined, down[...]).astype(BF)
    pre = dot(joined, base[...]) + dot(low, up[...])
    sigma = sigmoid(pre)
    new_out[...] = (feats[...].astype(F32) + pre * sigma).astype(BF)
    cot_wide = cot[...].astype(F32)
    slope = (cot_wide * (sigma * (1.0 + pre * (1.0 - sigma)))).astype(BF)
    mix = times_transposed(slope, up[...]).astype(BF)
    joined_grad = times_transposed(slope, base[...]) + times_transposed(mix, down[...])
    full = feats.shape[1]
    partial_out[...] = cot_wide + joined_grad[:, :full]
    agg_grad = joined_grad[:, full:].astype(BF)
    for i in range(pieces.shape[0]):
        q = (i // n_col) * 2 + (i >> 1) % 2
        pieces[i] = agg_grad[:, q * width : (q + 1) * width]
    grads[:, : 2 * full] = across(mix, joined)
    grads[:, 2 * full :] = across(low, slope)


def edge_kernel(feats, parts, pre, low, partial, base, down, up, feat_out, grads):
    width = parts.shape[-1]
    quarters = []
    for q in range(4):
        value = None
        for i in range(parts.shape[0] // 4):
            term = parts[i * 4 + q].astype(F32)
            value = term if value is None else value + term
        quarters.append(value)
    slopes = []
    for q in range(4):
        slopes.append((quarters[q] * silu_slope(pre[:, q * width : (q + 1) * width])).astype(BF))
    slope = jnp.concatenate(slopes, axis=1)
    mix = times_transposed(slope, up[...]).astype(BF)
    full = feats.shape[1]
    grads[:, :full] = across(mix, feats[...])
    grads[:, full:] = across(low[...], slope)
    feat_out[...] = (
        partial[...] + times_transposed(slope, base[...]) + times_transposed(mix, down[...])
    ).astype(BF)


def exchange(pieces, axes):
    shape = pieces.shape
    flat = pieces.reshape(shape[0] * shape[1], shape[2])
    return lax.all_to_all(flat, axes, split_axis=0, concat_axis=0, tiled=True)


def sum_over_all(grads, n_row, n_col):
    rank, wide = grads.shape
    lines = -(-wide // 1024) * 8
    part = rank // n_row * lines
    grads = jnp.pad(grads, ((0, 0), (0, lines * 128 - wide)))
    mine = exchange(grads.reshape(n_row, part, 128), ROW)
    mine = mine.reshape(n_row, part, 128).sum(axis=0)
    spread = jnp.broadcast_to(mine[None], (n_col, part, 128))
    mine = exchange(spread, COL).reshape(n_col, part, 128).sum(axis=0)
    spread = jnp.broadcast_to(mine[None], (n_row, part, 128))
    whole = exchange(spread, ROW).reshape(rank, lines * 128)
    return whole[:, :wide]


def body(
    node_feats,
    cotangent,
    edge_base,
    edge_down,
    edge_up,
    node_base,
    node_down,
    node_up,
    tile_weight,
    tile_place,
    tile_count,
):
    nodes, full = node_feats.shape
    n_row = lax.axis_size(ROW)
    n_col = lax.axis_size(COL)
    rank = edge_up.shape[0]
    width = full // 4
    tiles = tile_weight[0, 0]
    slots = tiles.shape[0]
    sds = jax.ShapeDtypeStruct

    def swap(values, axis):
        return lax.ppermute(values, axis, [(0, 1), (1, 0)])

    tiles_z = swap(tiles, "zl")
    tiles_c = swap(tiles, "co")
    tiles_cz = swap(tiles_z, "co")
    meta = jnp.concatenate([tile_place.reshape(1, 2 * slots), tile_count.reshape(1, 1)], axis=1)
    meta = jnp.pad(meta, ((0, 0), (0, 256 - meta.shape[1])))
    meta = lax.all_gather(meta, ("co", "zl"), axis=0, tiled=True)
    here = jnp.stack([lax.axis_index("co"), lax.axis_index("zl")]).astype(jnp.int32)

    pieces, pre, low = call(
        message_kernel,
        (
            sds((2 * n_row, nodes, width), BF),
            sds((nodes, full), F32),
            sds((nodes, rank), BF),
        ),
        node_feats,
        edge_base,
        edge_down,
        edge_up,
        name="message",
    )
    source = exchange(pieces, ROW_GROUP)

    def tile_sum(backward, values, rows):
        def kernel(*refs):
            tile_kernel(backward, *refs)

        return call(
            kernel,
            sds((rows, width), BF),
            here,
            meta,
            tiles,
            tiles_c,
            tiles_z,
            tiles_cz,
            values,
            scratch=[pltpu.VMEM((rows + 128, width), F32)],
            smem=2,
            flops=2 * 4 * slots * 128 * 128 * width,
            name="tiles_back" if backward else "tiles",
        )

    partial_rows = tile_sum(False, source, 2 * n_col * nodes)
    parts = lax.all_to_all(partial_rows, COL_GROUP, split_axis=0, concat_axis=0, tiled=True)
    new_feats, pieces, partial_grad, node_grads = call(
        node_kernel,
        (
            sds((nodes, full), BF),
            sds((2 * n_col, nodes, width), BF),
            sds((nodes, full), F32),
            sds((rank, 3 * full), F32),
        ),
        node_feats,
        cotangent,
        parts.reshape(2 * n_col, nodes, width),
        node_base,
        node_down,
        node_up,
        name="node",
    )
    source = exchange(pieces, COL_GROUP)
    partial_cols = tile_sum(True, source, 2 * n_row * nodes)
    parts = lax.all_to_all(partial_cols, ROW_GROUP, split_axis=0, concat_axis=0, tiled=True)
    feat_grad, edge_grads = call(
        edge_kernel,
        (sds((nodes, full), BF), sds((rank, 2 * full), F32)),
        node_feats,
        parts.reshape(2 * n_row, nodes, width),
        pre,
        low,
        partial_grad,
        edge_base,
        edge_down,
        edge_up,
        name="edge",
    )
    grads = sum_over_all(jnp.concatenate([edge_grads, node_grads], axis=1), n_row, n_col)
    grads = grads * (1.0 / math.sqrt(nodes * n_row * n_col))
    return (
        new_feats,
        feat_grad,
        grads[:, :full].T,
        grads[:, full : 2 * full],
        grads[:, 2 * full : 4 * full].T,
        grads[:, 4 * full :],
    )


def solution(mesh):
    n_row, n_col = mesh.shape["row"], mesh.shape["col"]
    fine = Mesh(mesh.devices.reshape(n_row // 2, 2, n_col // 4, 2, 2), ALL)
    nodes = P(ROW + COL, None)
    placed = (
        nodes,
        nodes,
        P(),
        P(),
        P(),
        P(),
        P(),
        P(),
        P(ROW, COL, None, None, None),
        P(ROW, COL, None, None),
        P(ROW, COL),
    )
    return jax.shard_map(
        body,
        mesh=fine,
        in_specs=placed,
        out_specs=(nodes, nodes, P(), P(), P(), P()),
        check_vma=False,
    )
```

time: 1030 us -> 297 us (0.29)
  waiting for transfers between devices: 827 us -> 80.7 us
  blocking collectives: 0 us -> 150 us
  other arithmetic: 79.4 us -> 0.15 us
  matrix products: 43.5 us -> 0 us
  local copies, waits for them, and re-layouts: 50.8 us -> 15.2 us
  starting transfers between devices: 0.25 us -> 24.8 us
  Pallas kernels: 0 us -> 23.6 us
  between operations: 22.7 us -> 1.51 us
    psum x2 -> x0, waiting for transfers between devices: 419 us -> none  [body(): lax.psum((across(node_feats, edge_mix), across(low_edge, edge_slope), acr...]
    reduce_scatter x2 -> x0, waiting for transfers between devices: 288 us -> none  [the longest x1 225 us: body(): lax.psum_scatter(partial_value.reshape(row_tiles * tile_size, feature_wid...]
    all_to_all x0 -> x5, blocking collectives: none -> 128 us  [the longest x4 94.3 us: exchange(): return lax.all_to_all(flat, axes, split_axis=0, concat_axis=0, tiled=True)]
    all_gather x2 -> x0, waiting for transfers between devices: 120 us -> none  [the longest x1 87.5 us: body(): lax.all_gather(agg_grad, 'col', axis=0, tiled=True)]
    scatter-add x6 -> x0, other arithmetic: 56 us -> none  [one_group(): carried.at[jnp.clip(other_part, 0, carried.shape[0] - 1)].add(products)]
    all_to_all x0 -> x2, waiting for transfers between devices: none -> 50.2 us  [the longest x1 50.2 us: body(): lax.all_to_all(partial_rows, COL_GROUP, split_axis=0, concat_axis=0, tile...]
    dot_general x22 -> x0, matrix products: 43.5 us -> none  [the longest x3 13.4 us: one_group(): jnp.einsum('gij,gjd->gid', weights_group, fetched, preferred_element_type...]
    gather x14 -> x0, local copies, waits for them, and re-layouts: 34 us -> none  [the longest x6 25 us: one_group(): fetched = pieces[jnp.clip(fetch_index, 0, pieces.shape[0] - 1)]]
  transfers between devices with their start and end apart: 6 -> 5, of which waited for: 6 -> 2; matrix products, arithmetic and copies ran while one was open for 9% -> 1% of each run, Pallas kernels for 0% -> 0%
where the time goes in v1:
time: 297 us; the launch traced here: 296 us
  blocking collectives  150 us (51%)
  waiting for transfers between devices  80.7 us (27%)
  starting transfers between devices  24.8 us (8%)
  Pallas kernels  23.6 us (8%)
  local copies, waits for them, and re-layouts  15.2 us (5%)
    all_to_all x4, blocking collectives, exchange(): return lax.all_to_all(flat, axes, split_axis=0, concat_axis=0, tiled=True)  94.3 us
    all_to_all x1, waiting for transfers between devices, body(): lax.all_to_all(partial_rows, COL_GROUP, split_axis=0, concat_axis=0, tile...  50.2 us
    all_to_all x1, blocking collectives, body(): lax.all_to_all(partial_cols, ROW_GROUP, split_axis=0, concat_axis=0, tile...  33.7 us
    ppermute x3, waiting for transfers between devices, swap(): return lax.ppermute(values, axis, [(0, 1), (1, 0)])  30.5 us
    pallas_call x5, Pallas kernels, call(): pl.pallas_call(kernel, out_shape=out_shape, in_specs=[pl.BlockSpec(memory...  23.6 us
    all_gather x1, blocking collectives, body(): meta = lax.all_gather(meta, ('co', 'zl'), axis=0, tiled=True)  21.6 us
    unnamed x45, local copies, waits for them, and re-layouts  13.8 us
    all_to_all x1, starting transfers between devices, body(): lax.all_to_all(partial_rows, COL_GROUP, split_axis=0, concat_axis=0, tile...  10.2 us
  transfers between devices with their start and end apart: 5, of which 2 were waited for; matrix products, arithmetic and copies ran while one was open for 1% of the time, Pallas kernels for 0%

profile of v1, /device:TPU:1, one launch (start us, length us, event | category | flops | bytes accessed | tf_op | source)
XLA Modules:
  0.0 295.5 jit_solution(18346348067072097935)
XLA Ops:
  0.6 2.6 collective-permute-start.1
  4.0 0.9 copy-done.3
  5.0 1.0 copy-done.6
  7.5 1.4 copy-done.5
  10.3 6.6 %all-to-all-start = ((bf16[32,256,128]{2,1,0:T(8,128)(2,1)}), bf16[32,256,128]{2,1,0:T(8,128)(2,1)S(1)}, u32[]{:S(2)}, u32[]{:S(2)}) async-start(bf16[32,256,128]{2,1,0:T(8,128)(2,1)} %copy-done.5), calls=%async_computation | async-start | bytes 4194304 | tf_op jit(solution)/shard_map/all_to_all | solution.py:173
  17.3 30.5 %collective-permute-done.1.refs_4_ = bf16[64,128,128]{2,1,0:T(8,128)(2,1)} collective-permute-done((bf16[64,128,128]{2,1,0:T(8,128)(2,1)}, bf16[64,128,128]{2,1,0:T(8,128)(2,1)}, u32[]{:S(2)}, u32[]{:S(2)}) %collective-permute-start.1) | collective-permute-done | bytes 2097184 | tf_op jit(solution)/shard_map/ppermute | solution.py:213
  47.8 5.0 %collective-permute-start.2 = (bf16[64,128,128]{2,1,0:T(8,128)(2,1)}, bf16[64,128,128]{2,1,0:T(8,128)(2,1)}, u32[]{:S(2)}, u32[]{:S(2)}) collective-permute-start(bf16[64,128,128]{2,1,0:T(8,128)(2,1)} %collective-permute-done.1.refs_4_), channel_id=1, source_target_pairs={{0,16},{16,0},{1,17},{17,1},{2,18},{18,2},{3,19},{19,3},{4,20},{20... | collective-permute-start | bytes 6291464 | tf_op jit(solution)/shard_map/ppermute | solution.py:213
  53.8 21.6 %all-gather = s32[4,1,256]{2,1,0:T(1,128)S(1)} all-gather(s32[1,1,256]{2,1,0:T(1,128)S(1)} %pad_bitcast_fusion), channel_id=1, replica_groups=mesh['xly'=8,'co'=2,'zh'=4,'zl'=2,'xh'=2] {'co','zl'}, dimensions={0}, use_global_device_ids=true | all-gather | bytes 5120 | tf_op jit(solution)/shard_map/all_gather | solution.py:220
  75.5 1.6 copy-done.1
  77.1 9.1 %tiles.1 = bf16[8192,128]{1,0:T(8,128)(2,1)S(1)} custom-call(s32[2]{0:T(128)S(1)} %pad_add_fusion.1.refs_0_, s32[4,256]{1,0:T(4,128)S(1)} %bitcast.33, bf16[64,128,128]{2,1,0:T(8,128)(2,1)S(1)} %bitcast.31, bf16[64,128,128]{2,1,0:T(8,128)(2,1)} %collective-permute-done.refs_3_, bf16[64,128,128]{2,1,0:T(8,128)(2,1)} %collective-permute-done.1.refs_4_, ...), custom_call_target="tpu_custom_call" | custom-call | flops 1073741824 | bytes 12587016 | tf_op jit(solution)/shard_map/tiles/pallas_call | solution.py:43
  86.2 1.4 copy-done
  87.5 10.2 %all-to-all-start.1 = ((bf16[32,256,128]{2,1,0:T(8,128)(2,1)}), bf16[32,256,128]{2,1,0:T(8,128)(2,1)S(1)}, u32[]{:S(2)}, u32[]{:S(2)}) async-start(bf16[32,256,128]{2,1,0:T(8,128)(2,1)} %bitcast.26), calls=%async_computation.1 | async-start | bytes 4194304 | tf_op jit(solution)/shard_map/all_to_all | solution.py:259
  97.8 1.6 copy.31.down
  99.4 50.2 %all-to-all-done.1.parts = bf16[32,256,128]{2,1,0:T(8,128)(2,1)S(1)} async-done(((bf16[32,256,128]{2,1,0:T(8,128)(2,1)}), bf16[32,256,128]{2,1,0:T(8,128)(2,1)S(1)}, u32[]{:S(2)}, u32[]{:S(2)}) %all-to-all-start.1) | async-done | bytes 2097184 | tf_op jit(solution)/shard_map/all_to_all | solution.py:259
  149.6 0.9 copy-done.9
  150.6 0.9 copy-done.12
  152.2 2.0 node.1
  154.3 55.7 %all_to_all.55 = bf16[32,256,128]{2,1,0:T(8,128)(2,1)S(1)} all-to-all(bf16[32,256,128]{2,1,0:T(8,128)(2,1)S(1)} %get-tuple-element.17), channel_id=1, replica_groups=mesh['xly'=8,'co'=2,'zh'=4,'zl'=2,'xh'=2] {'co','zh','zl','xh'}, dimensions={0} | all-to-all | bytes 4194304 | tf_op jit(solution)/shard_map/all_to_all | solution.py:173
  210.0 10.0 %tiles_back.1 = bf16[8192,128]{1,0:T(8,128)(2,1)S(1)} custom-call(s32[2]{0:T(128)S(1)} %pad_add_fusion.1.refs_0_, s32[4,256]{1,0:T(4,128)S(1)} %bitcast.34, bf16[64,128,128]{2,1,0:T(8,128)(2,1)S(1)} %bitcast.32, bf16[64,128,128]{2,1,0:T(8,128)(2,1)} %collective-permute-done.refs_3_, bf16[64,128,128]{2,1,0:T(8,128)(2,1)} %collective-permute-done.1.refs_4_, ...), custom_call_target="tpu_custom_call" | custom-call | flops 1073741824 | bytes 12587016 | tf_op jit(solution)/shard_map/tiles_back/pallas_call | solution.py:43
  220.1 33.7 %all_to_all.56.parts = bf16[32,256,128]{2,1,0:T(8,128)(2,1)S(1)} all-to-all(bf16[32,256,128]{2,1,0:T(8,128)(2,1)S(1)} %bitcast.28), channel_id=1, replica_groups=mesh['xly'=8,'co'=2,'zh'=4,'zl'=2,'xh'=2] {'xly','co','zl'}, dimensions={0} | all-to-all | bytes 4194304 | tf_op jit(solution)/shard_map/all_to_all | solution.py:278
  253.8 1.8 edge.1
  255.6 10.3 %all_to_all.57 = f32[16,24,128]{2,1,0:T(8,128)S(1)} all-to-all(f32[16,24,128]{2,1,0:T(8,128)S(1)} %bitcast.35), channel_id=1, replica_groups=mesh['xly'=8,'co'=2,'zh'=4,'zl'=2,'xh'=2] {'xly','co'}, dimensions={0} | all-to-all | bytes 393216 | tf_op jit(solution)/shard_map/all_to_all | solution.py:173
  266.0 16.4 %all_to_all.58 = f32[16,24,128]{2,1,0:T(8,128)S(1)} all-to-all(f32[16,24,128]{2,1,0:T(8,128)S(1)} %broadcast_in_dim.4), channel_id=1, replica_groups=mesh['xly'=8,'co'=2,'zh'=4,'zl'=2,'xh'=2] {'zh','zl','xh'}, dimensions={0} | all-to-all | bytes 393216 | tf_op jit(solution)/shard_map/all_to_all | solution.py:173
  282.4 11.8 %all_to_all.59 = f32[16,24,128]{2,1,0:T(8,128)S(1)} all-to-all(f32[16,24,128]{2,1,0:T(8,128)S(1)} %broadcast_in_dim.5), channel_id=1, replica_groups=mesh['xly'=8,'co'=2,'zh'=4,'zl'=2,'xh'=2] {'xly','co'}, dimensions={0} | all-to-all | bytes 393216 | tf_op jit(solution)/shard_map/all_to_all | solution.py:173
  (53 shorter events, 6.6 us)
Async XLA Ops:
  0.6 47.2 %collective-permute-start.1 = (bf16[64,128,128]{2,1,0:T(8,128)(2,1)}, bf16[64,128,128]{2,1,0:T(8,128)(2,1)}, u32[]{:S(2)}, u32[]{:S(2)}) collective-permute-start(bf16[64,128,128]{2,1,0:T(8,128)(2,1)} %bitcast.29), channel_id=1, source_target_pairs={{0,2},{2,0},{1,3},{3,1},{4,6},{6,4},{5,7},{7,5},{8,10},{10,8},{9,1... | collective-permute-start | bytes 6291464 | tf_op jit(solution)/shard_map/ppermute | solution.py:213
  4.0 1.0 copy-start.3
  5.0 1.0 copy-start.6
  6.0 0.7 copy-start.15
  7.5 1.4 copy-start.5
  8.8 0.9 copy-start.10
  9.7 0.6 copy-start.13
  10.3 43.2 %copy-start.18 = (s32[1,1,64,2]{2,3,1,0:T(2,128)S(1)}, s32[1,1,64,2]{2,3,1,0:T(2,128)}, u32[]{:S(2)}) copy-start(s32[1,1,64,2]{2,3,1,0:T(2,128)} %param.20) | copy-start | bytes 1540
  10.3 65.1 %all-to-all-start = ((bf16[32,256,128]{2,1,0:T(8,128)(2,1)}), bf16[32,256,128]{2,1,0:T(8,128)(2,1)S(1)}, u32[]{:S(2)}, u32[]{:S(2)}) async-start(bf16[32,256,128]{2,1,0:T(8,128)(2,1)} %copy-done.5), calls=%async_computation | async-start | bytes 4194304 | tf_op jit(solution)/shard_map/all_to_all | solution.py:173
  17.0 58.5 %collective-permute-start = (bf16[64,128,128]{2,1,0:T(8,128)(2,1)}, bf16[64,128,128]{2,1,0:T(8,128)(2,1)}, u32[]{:S(2)}, u32[]{:S(2)}) collective-permute-start(bf16[64,128,128]{2,1,0:T(8,128)(2,1)} %bitcast.30), channel_id=1, source_target_pairs={{0,16},{16,0},{1,17},{17,1},{2,18},{18,2},{3,19},{19,3},{4,20},{20... | collective-permute-start | bytes 6291464 | tf_op jit(solution)/shard_map/ppermute | solution.py:213
  47.8 27.7 %collective-permute-start.2 = (bf16[64,128,128]{2,1,0:T(8,128)(2,1)}, bf16[64,128,128]{2,1,0:T(8,128)(2,1)}, u32[]{:S(2)}, u32[]{:S(2)}) collective-permute-start(bf16[64,128,128]{2,1,0:T(8,128)(2,1)} %collective-permute-done.1.refs_4_), channel_id=1, source_target_pairs={{0,16},{16,0},{1,17},{17,1},{2,18},{18,2},{3,19},{19,3},{4,20},{20... | collective-permute-start | bytes 6291464 | tf_op jit(solution)/shard_map/ppermute | solution.py:213
  75.5 1.6 copy-start.1
  86.2 1.4 copy-start
  87.5 62.1 %copy-start.4 = (bf16[256,512]{1,0:T(8,128)(2,1)S(1)}, bf16[256,512]{1,0:T(8,128)(2,1)}, u32[]{:S(2)}) copy-start(bf16[256,512]{1,0:T(8,128)(2,1)} %feats.5) | copy-start | bytes 786436
  87.5 62.1 %copy-start.8 = (bf16[1024,512]{1,0:T(8,128)(2,1)S(1)}, bf16[1024,512]{1,0:T(8,128)(2,1)}, u32[]{:S(2)}) copy-start(bf16[1024,512]{1,0:T(8,128)(2,1)} %base.4) | copy-start | bytes 3145732
  87.5 62.0 %all-to-all-start.1 = ((bf16[32,256,128]{2,1,0:T(8,128)(2,1)}), bf16[32,256,128]{2,1,0:T(8,128)(2,1)S(1)}, u32[]{:S(2)}, u32[]{:S(2)}) async-start(bf16[32,256,128]{2,1,0:T(8,128)(2,1)} %bitcast.26), calls=%async_computation.1 | async-start | bytes 4194304 | tf_op jit(solution)/shard_map/all_to_all | solution.py:259
  149.6 1.0 copy-start.9
  150.6 0.9 copy-start.12
  151.5 0.7 copy-start.17
  154.2 55.8 %copy-start.2 = (bf16[1,1,64,128,128]{4,3,2,1,0:T(8,128)(2,1)S(1)}, bf16[1,1,64,128,128]{4,3,2,1,0:T(8,128)(2,1)}, u32[]{:S(2)}) copy-start(bf16[1,1,64,128,128]{4,3,2,1,0:T(8,128)(2,1)} %param.19) | copy-start | bytes 6291460
  220.0 33.7 %copy-start.7 = (bf16[512,512]{1,0:T(8,128)(2,1)S(1)}, bf16[512,512]{1,0:T(8,128)(2,1)}, u32[]{:S(2)}) copy-start(bf16[512,512]{1,0:T(8,128)(2,1)} %base.5) | copy-start | bytes 1572868
  220.0 33.7 %copy-start.11 = (f32[256,512]{1,0:T(8,128)S(1)}, f32[256,512]{1,0:T(8,128)}, u32[]{:S(2)}) copy-start(f32[256,512]{1,0:T(8,128)} %copy-done.10) | copy-start | bytes 1572868
  220.0 33.7 %copy-start.14 = (bf16[256,16]{1,0:T(8,128)(2,1)S(1)}, bf16[256,16]{1,0:T(8,128)(2,1)}, u32[]{:S(2)}) copy-start(bf16[256,16]{1,0:T(8,128)(2,1)} %copy-done.13) | copy-start | bytes 24580
  220.1 33.7 %copy-start.16 = (bf16[16,512]{1,0:T(8,128)(2,1)S(1)}, bf16[16,512]{1,0:T(8,128)(2,1)}, u32[]{:S(2)}) copy-start(bf16[16,512]{1,0:T(8,128)(2,1)} %up.5) | copy-start | bytes 49156

commit v2 on v1

v2 whole, which is shorter than its diff:
```python
import math

import jax
import jax.numpy as jnp
from jax import lax
from jax.experimental import pallas as pl
from jax.experimental.pallas import tpu as pltpu
from jax.sharding import Mesh, PartitionSpec as P

BF, F32 = jnp.bfloat16, jnp.float32
UNROLL = 8
PARTS = 4
MIB = 1 << 20
ALL = ("xly", "co", "z", "xh")
ROW, COL = ("xly", "co"), ("z", "xh")


def dot(left, right):
    return jnp.dot(left, right, preferred_element_type=F32)


def across(left, right):
    return lax.dot_general(left, right, (((0,), (0,)), ((), ())), preferred_element_type=F32)


def times_transposed(left, right):
    return lax.dot_general(left, right, (((1,), (1,)), ((), ())), preferred_element_type=F32)


def sigmoid(values):
    return 1.0 / (1.0 + jnp.exp(-values))


def silu_slope(values):
    sigma = sigmoid(values)
    return sigma * (1.0 + values * (1.0 - sigma))


def call(kernel, out_shape, *args, scratch=(), smem=0, vmem=40, flops=0, name=None, far=()):
    def place(i):
        return pl.BlockSpec(memory_space=pltpu.HBM if i in far else pltpu.VMEM)

    moved = sum(a.size * a.dtype.itemsize for a in args)
    moved += sum(math.prod(s.shape) * s.dtype.itemsize for s in jax.tree.leaves(out_shape))
    return pl.pallas_call(
        kernel,
        out_shape=out_shape,
        in_specs=[pl.BlockSpec(memory_space=pltpu.SMEM)] * smem
        + [place(i) for i in range(smem, len(args))],
        out_specs=(pl.BlockSpec(memory_space=pltpu.VMEM),) * len(out_shape),
        scratch_shapes=list(scratch),
        compiler_params=pltpu.CompilerParams(vmem_limit_bytes=vmem * MIB),
        cost_estimate=pl.CostEstimate(flops=flops, bytes_accessed=moved, transcendentals=0),
        name=name,
    )(*args)


def add(*terms):
    total = terms[0].astype(F32)
    for term in terms[1:]:
        total = total + term.astype(F32)
    return total


def message_kernel(feats, base, down_t, up, pieces):
    low = times_transposed(feats[...], down_t[...]).astype(BF)
    pre = dot(feats[...], base[...]) + dot(low, up[...])
    message = (pre * sigmoid(pre)).astype(BF)
    width = pieces.shape[2]
    for i in range(pieces.shape[0]):
        pieces[i] = message[:, i % 2 * width : (i % 2 + 1) * width]


def clear(total):
    rows = total.shape[0] - 128

    def step(i, carry):
        at = pl.ds(pl.multiple_of(i * 256, 256), 256)
        total[at, :] = jnp.zeros((256, total.shape[1]), F32)
        return carry

    lax.fori_loop(0, rows // 256, step, 0)


def fetch_tiles(stacks, near, sems):
    size = near.shape[1] // PARTS
    copies = []
    for owner, stack in enumerate(stacks):
        for part in range(PARTS):
            at = pl.ds(part * size, size)
            copy = pltpu.make_async_copy(
                stack.at[at], near.at[owner, at], sems.at[owner * PARTS + part]
            )
            copy.start()
            copies.append(copy)
    return copies


def add_tiles(meta, owner, weights, copies, source, source_at, total, backward):
    slots = weights.shape[0]
    spare = total.shape[0] - 128
    count = meta[owner, 2 * slots]
    size = slots // PARTS

    def group(i, carry):
        products, places = [], []
        for j in range(UNROLL):
            slot = i * UNROLL + j
            live = slot < count
            tile_row = jnp.where(live, meta[owner, 2 * slot], 0)
            tile_col = jnp.where(live, meta[owner, 2 * slot + 1], 0)
            from_tile, to_tile = (tile_row, tile_col) if backward else (tile_col, tile_row)
            places.append(pl.multiple_of(jnp.where(live, to_tile * 128, spare), 128))
            block = source[pl.ds(pl.multiple_of(source_at + from_tile * 128, 128), 128), :]
            tile = weights[slot]
            products.append(across(tile, block) if backward else dot(tile, block))
        for product, at in zip(products, places):
            total[pl.ds(at, 128), :] += product
        return carry

    for part, copy in enumerate(copies):
        copy.wait()
        end = jnp.minimum(count, (part + 1) * size)
        lax.fori_loop(part * size // UNROLL, (end + UNROLL - 1) // UNROLL, group, 0)


def forward_kernel(owner, groups, n_z, here, meta, stack, source, *rest):
    outs, (total, near, sems) = rest[:-3], rest[-3:]
    copies = fetch_tiles([stack], near, sems)
    z, xh = here[1], here[2]
    nodes = (total.shape[0] - 128) // (2 * n_z)
    clear(total)
    add_tiles(meta, owner, near.at[0], copies, source, 0, total, False)
    for out, places in zip(outs, groups):
        for k, (distance, side) in enumerate(places):
            to = lax.rem(z + (distance + n_z), n_z) * 2 + (xh ^ side)
            block = total[pl.ds(pl.multiple_of(to * nodes, nodes), nodes), :]
            out[k * nodes : (k + 1) * nodes] = block.astype(BF)


def backward_kernel(places, n_z, here, meta, stack, stack_other, *rest):
    shards, (out, total, source, near, sems) = rest[:-5], rest[-5:]
    copies = fetch_tiles([stack, stack_other], near, sems)
    z, xh = here[1], here[2]
    nodes = source.shape[0] // (4 * n_z)
    for shard, wanted in zip(shards, places):
        for k, (owner, distance, side) in enumerate(wanted):
            at = (owner * n_z + lax.rem(z + (distance + n_z), n_z)) * 2 + (xh ^ side)
            source[pl.ds(pl.multiple_of(at * nodes, nodes), nodes), :] = shard[
                k * nodes : (k + 1) * nodes
            ]
    clear(total)
    add_tiles(meta, 0, near.at[0], copies[:PARTS], source, 0, total, True)
    add_tiles(meta, 1, near.at[1], copies[PARTS:], source, 2 * n_z * nodes, total, True)

    def finish(i, carry):
        at = pl.ds(pl.multiple_of(i * 256, 256), 256)
        out[at, :] = total[at, :].astype(BF)
        return carry

    lax.fori_loop(0, out.shape[0] // 256, finish, 0)


def node_kernel(here, feats, cot, t0, t1, t2, t3, other, base, down_t, up, new_out, keep, give, partial_out, grads):
    first = here[0] == 0
    full = feats.shape[1]
    half = full // 2
    nodes = feats.shape[0]
    mine = add(t0[:nodes], t1[:nodes], t2[:nodes], t3[...]).astype(BF)
    rest = other[...]
    agg = [jnp.where(first, mine, rest), jnp.where(first, rest, mine)]
    joined = jnp.concatenate([feats[...]] + agg, axis=1)
    low = times_transposed(joined, down_t[...]).astype(BF)
    pre = dot(joined, base[...]) + dot(low, up[...])
    sigma = sigmoid(pre)
    cot_wide = cot[...].astype(F32)
    slope = (cot_wide * (sigma * (1.0 + pre * (1.0 - sigma)))).astype(BF)
    mix = times_transposed(slope, up[...]).astype(BF)
    joined_grad = times_transposed(slope, base[...]) + dot(mix, down_t[...])
    agg_grad = joined_grad[:, full:].astype(BF)
    keep[...] = jnp.where(first, agg_grad[:, :half], agg_grad[:, half:])
    give[...] = jnp.where(first, agg_grad[:, half:], agg_grad[:, :half])
    new_out[...] = (feats[...].astype(F32) + pre * sigma).astype(BF)
    partial_out[...] = cot_wide + joined_grad[:, :full]
    grads[:, : 2 * full] = across(mix, joined)
    grads[:, 2 * full :] = across(low, slope)


def edge_kernel(feats, parts, partial, base, down_t, up, feat_out, grads):
    full = feats.shape[1]
    low = times_transposed(feats[...], down_t[...]).astype(BF)
    pre = dot(feats[...], base[...]) + dot(low, up[...])
    factor = silu_slope(pre)
    halves = [None] * 2
    for i in range(parts.shape[0]):
        term = parts[i].astype(F32)
        halves[i % 2] = term if halves[i % 2] is None else halves[i % 2] + term
    slope = (jnp.concatenate(halves, axis=1) * factor).astype(BF)
    mix = times_transposed(slope, up[...]).astype(BF)
    grads[:, :full] = across(mix, feats[...])
    grads[:, full:] = across(low, slope)
    feat_out[...] = (
        partial[...] + times_transposed(slope, base[...]) + dot(mix, down_t[...])
    ).astype(BF)


def exchange(pieces, axes):
    shape = pieces.shape
    flat = pieces.reshape(shape[0] * shape[1], shape[2])
    return lax.all_to_all(flat, axes, split_axis=0, concat_axis=0, tiled=True)


def sum_over_all(grads):
    near = ("xly", "co", "xh")
    n_near, n_z = lax.axis_size(near), lax.axis_size("z")
    rank, wide = grads.shape
    lines = -(-rank * wide // (n_near * 1024)) * 8
    grads = jnp.pad(grads.reshape(-1), (0, n_near * lines * 128 - rank * wide))
    mine = exchange(grads.reshape(n_near, lines, 128), near)
    mine = mine.reshape(n_near, lines, 128).sum(axis=0)
    spread = jnp.broadcast_to(mine[None], (n_z, lines, 128))
    mine = exchange(spread, "z").reshape(n_z, lines, 128).sum(axis=0)
    spread = jnp.broadcast_to(mine[None], (n_near, lines, 128))
    whole = exchange(spread, near).reshape(-1)
    return whole[: rank * wide].reshape(rank, wide)


def body(
    node_feats,
    cotangent,
    edge_base,
    edge_down,
    edge_up,
    node_base,
    node_down,
    node_up,
    tile_weight,
    tile_place,
    tile_count,
):
    nodes, full = node_feats.shape
    n_row = lax.axis_size(ROW)
    n_col = lax.axis_size(COL)
    n_z = lax.axis_size("z")
    n_up, n_down = n_z // 2, (n_z - 1) // 2
    rank = edge_up.shape[0]
    half = full // 2
    tiles = tile_weight[0, 0]
    slots = tiles.shape[0]
    sds = jax.ShapeDtypeStruct

    def swap(values, axis):
        return lax.ppermute(values, axis, [(0, 1), (1, 0)])

    def up(values):
        return lax.ppermute(values, "z", [(i, (i + 1) % n_z) for i in range(n_z)])

    def down(values):
        return lax.ppermute(values, "z", [((i + 1) % n_z, i) for i in range(n_z)])

    meta = jnp.concatenate([tile_place.reshape(1, 2 * slots), tile_count.reshape(1, 1)], axis=1)
    meta = jnp.pad(meta, ((0, 0), (0, 256 - meta.shape[1])))
    meta = jnp.concatenate([meta, swap(meta, "co")], axis=0)
    tiles_c = swap(tiles, "co")
    here = jnp.stack([lax.axis_index("co"), lax.axis_index("z"), lax.axis_index("xh")])
    here = here.astype(jnp.int32)

    pieces = call(
        message_kernel,
        (sds((n_row, nodes, half), BF),),
        node_feats,
        edge_base,
        edge_down.T,
        edge_up,
        name="message",
    )[0]
    source = exchange(pieces, ROW)

    def forward_sum(owner, weights, source, groups, name):
        rows = n_col * nodes

        def kernel(*refs):
            forward_kernel(owner, groups, n_z, *refs)

        return call(
            kernel,
            tuple(sds((len(places) * nodes, half), BF) for places in groups),
            here,
            meta,
            weights,
            source,
            scratch=[
                pltpu.VMEM((rows + 128, half), F32),
                pltpu.VMEM((1, slots, 128, 128), BF),
                pltpu.SemaphoreType.DMA((PARTS,)),
            ],
            smem=2,
            far=(2,),
            flops=2 * slots * 128 * 128 * half,
            name=name,
        )

    flat = [d for i in range(n_up) for d in (n_up - i, i - n_down)]
    pairs = [flat[: n_z // 2], flat[n_z // 2 :]]
    outs = forward_sum(
        1, tiles_c, source, [[(d, 1) for d in group] for group in pairs] + [[(d, 0)] for d in flat], "tiles_other"
    )
    kept = dict(zip(flat, outs[2:]))
    other = {}
    for group, sent in zip(pairs, outs[:2]):
        got = swap(sent, "xh")
        for k, d in enumerate(group):
            other[d] = add(kept[d], got[k * nodes : (k + 1) * nodes]).astype(BF)
    source = lax.optimization_barrier((source,) + tuple(outs[:2]))[0]
    outs = forward_sum(0, tiles, source, [[(d, 0), (d, 1)] for d in flat], "tiles_own")
    own = dict(zip(flat, outs))

    def ring_sum(blocks):
        rising = up(blocks[n_up])
        falling = down(blocks[-n_down]) if n_down else None
        for k in range(1, n_up):
            rising = up(add(rising, blocks[n_up - k]).astype(BF))
            if k < n_down:
                falling = down(add(falling, blocks[k - n_down]).astype(BF))
        return [blocks[0], rising] + ([falling] if n_down else [])

    other_terms = ring_sum(other)
    own_terms = ring_sum(own)
    agg_other = swap(add(*other_terms).astype(BF), "co")
    across_x = swap(add(*[term[nodes:] for term in own_terms]).astype(BF), "xh")
    if not n_down:
        own_terms = own_terms + [jnp.zeros_like(own_terms[0])]
    new_feats, keep, give, partial_grad, node_grads = call(
        node_kernel,
        (
            sds((nodes, full), BF),
            sds((nodes, half), BF),
            sds((nodes, half), BF),
            sds((nodes, full), F32),
            sds((rank, 3 * full), F32),
        ),
        here,
        node_feats,
        cotangent,
        *own_terms,
        across_x,
        agg_other,
        node_base,
        node_down.T,
        node_up,
        smem=1,
        name="node",
    )

    def ring_gather(block):
        blocks = {0: block}
        for k in range(1, n_up + 1):
            blocks[-k] = up(blocks[1 - k])
            if k <= n_down:
                blocks[k] = down(blocks[k - 1])
        return blocks

    own = ring_gather(jnp.concatenate([keep, swap(keep, "xh")], axis=0))
    other = ring_gather(swap(give, "co"))
    shards, places = [], []
    for d in own:
        shards.append(own[d])
        places.append([(0, d, 0), (0, d, 1)])
    groups = [[0, -1] if n_down < 1 else [0, 1, -1]] + [[k, -k] for k in range(2, n_down + 1)]
    if n_up > max(1, n_down):
        groups.append([-n_up])
    for group in groups:
        shards += [other[d] for d in group]
        places += [[(1, d, 0)] for d in group]
        shards.append(swap(jnp.concatenate([other[d] for d in group]), "xh"))
        places.append([(1, d, 1) for d in group])

    def backward(*refs):
        backward_kernel(places, n_z, *refs)

    rows = n_row * nodes
    partial_cols = call(
        backward,
        (sds((rows, half), BF),),
        here,
        meta,
        tiles,
        tiles_c,
        *shards,
        scratch=[
            pltpu.VMEM((rows + 128, half), F32),
            pltpu.VMEM((2 * n_col * nodes, half), BF),
            pltpu.VMEM((2, slots, 128, 128), BF),
            pltpu.SemaphoreType.DMA((2 * PARTS,)),
        ],
        smem=2,
        far=(2, 3),
        flops=4 * slots * 128 * 128 * half,
        name="tiles_back",
    )[0]
    parts = lax.all_to_all(partial_cols, ROW, split_axis=0, concat_axis=0, tiled=True)
    feat_grad, edge_grads = call(
        edge_kernel,
        (sds((nodes, full), BF), sds((rank, 2 * full), F32)),
        node_feats,
        parts.reshape(n_row, nodes, half),
        partial_grad,
        edge_base,
        edge_down.T,
        edge_up,
        name="edge",
    )
    grads = sum_over_all(jnp.concatenate([edge_grads, node_grads], axis=1))
    grads = grads * (1.0 / math.sqrt(nodes * n_row * n_col))
    return (
        new_feats,
        feat_grad,
        grads[:, :full].T,
        grads[:, full : 2 * full],
        grads[:, 2 * full : 4 * full].T,
        grads[:, 4 * full :],
    )


def solution(mesh):
    n_row, n_col = mesh.shape["row"], mesh.shape["col"]
    fine = Mesh(mesh.devices.reshape(n_row // 2, 2, n_col // 2, 2), ALL)
    nodes = P(ROW + COL, None)
    placed = (
        nodes,
        nodes,
        P(),
        P(),
        P(),
        P(),
        P(),
        P(),
        P(ROW, COL, None, None, None),
        P(ROW, COL, None, None),
        P(ROW, COL),
    )
    return jax.shard_map(
        body,
        mesh=fine,
        in_specs=placed,
        out_specs=(nodes, nodes, P(), P(), P(), P()),
        check_vma=False,
    )
```

time: 297 us -> 257 us (0.87); the launches traced: 296 us -> 252 us
  blocking collectives: 150 us -> 81 us
  starting transfers between devices: 24.8 us -> 82.4 us
  waiting for transfers between devices: 80.7 us -> 61.7 us
  local copies, waits for them, and re-layouts: 15.2 us -> 6.44 us
  Pallas kernels: 23.6 us -> 18.1 us
    ppermute x0 -> x28, starting transfers between devices: none -> 51.5 us  [the longest x16 31.8 us: up(): return lax.ppermute(values, 'z', [(i, (i + 1) % n_z) for i in range(n_z)])]
    all_to_all x4 -> x3, blocking collectives: 94.3 us -> 43.1 us  [exchange(): return lax.all_to_all(flat, axes, split_axis=0, concat_axis=0, tiled=True)]
    all_to_all x1 -> x0, waiting for transfers between devices: 50.2 us -> none  [body(): lax.all_to_all(partial_rows, COL_GROUP, split_axis=0, concat_axis=0, tile...]
    all_to_all x1, waiting for transfers between devices: 0.01 us -> 25.8 us  [exchange(): return lax.all_to_all(flat, axes, split_axis=0, concat_axis=0, tiled=True)]
    ppermute x0 -> x28, waiting for transfers between devices: none -> 23.8 us  [the longest x16 22.2 us: up(): return lax.ppermute(values, 'z', [(i, (i + 1) % n_z) for i in range(n_z)])]
    all_gather x1 -> x0, blocking collectives: 21.6 us -> none  [body(): meta = lax.all_gather(meta, ('co', 'zl'), axis=0, tiled=True)]
    ppermute x3 -> x12, starting transfers between devices: 7.92 us -> 26.9 us  [swap(): return lax.ppermute(values, axis, [(0, 1), (1, 0)])]
    ppermute x3 -> x12, waiting for transfers between devices: 30.5 us -> 12.1 us  [swap(): return lax.ppermute(values, axis, [(0, 1), (1, 0)])]
  transfers between devices with their start and end apart: 5 -> 41, of which waited for: 2 -> 17; matrix products, arithmetic and copies ran while one was open for 1% -> 0% of each run, Pallas kernels for 0% -> 0%
where the time goes in v2:
time: 257 us; the launch traced here: 252 us
  starting transfers between devices  82.4 us (32%)
  blocking collectives  81 us (32%)
  waiting for transfers between devices  61.7 us (24%)
  Pallas kernels  18.1 us (7%)
  local copies, waits for them, and re-layouts  6.44 us (3%)
    all_to_all x3, blocking collectives, exchange(): return lax.all_to_all(flat, axes, split_axis=0, concat_axis=0, tiled=True)  43.1 us
    all_to_all x1, blocking collectives, body(): lax.all_to_all(partial_cols, ROW, split_axis=0, concat_axis=0, tiled=True)  37.9 us
    ppermute x16, starting transfers between devices, up(): return lax.ppermute(values, 'z', [(i, (i + 1) % n_z) for i in range(n_z)])  31.8 us
    ppermute x12, starting transfers between devices, swap(): return lax.ppermute(values, axis, [(0, 1), (1, 0)])  26.9 us
    all_to_all x1, waiting for transfers between devices, exchange(): return lax.all_to_all(flat, axes, split_axis=0, concat_axis=0, tiled=True)  25.8 us
    ppermute x16, waiting for transfers between devices, up(): return lax.ppermute(values, 'z', [(i, (i + 1) % n_z) for i in range(n_z)])  22.2 us
    ppermute x12, starting transfers between devices, down(): return lax.ppermute(values, 'z', [((i + 1) % n_z, i) for i in range(n_z)])  19.7 us
    pallas_call x6, Pallas kernels, call(): pl.pallas_call(kernel, out_shape=out_shape, in_specs=[pl.BlockSpec(memory...  18.1 us
  transfers between devices with their start and end apart: 41, of which 17 were waited for; matrix products, arithmetic and copies ran while one was open for 0% of the time, Pallas kernels for 0%

profile of v2, /device:TPU:1, one launch (start us, length us, event | category | flops | bytes accessed | tf_op | source)
XLA Modules:
  0.0 252.4 jit_solution(9595378748821796965)
XLA Ops:
  0.6 3.3 %collective-permute-start.1 = (bf16[64,128,128]{2,1,0:T(8,128)(2,1)}, bf16[64,128,128]{2,1,0:T(8,128)(2,1)}, u32[]{:S(2)}, u32[]{:S(2)}) collective-permute-start(bf16[64,128,128]{2,1,0:T(8,128)(2,1)} %bitcast.17), channel_id=1, source_target_pairs={{0,16},{16,0},{1,17},{17,1},{2,18},{18,2},{3,19},{19,3},{4,20},{20... | collective-permute-start | bytes 6291464 | tf_op jit(solution)/shard_map/ppermute | solution.py:253
  9.4 3.9 %all-to-all-start = ((bf16[16,256,256]{2,1,0:T(8,128)(2,1)}), bf16[16,256,256]{2,1,0:T(8,128)(2,1)S(1)}, u32[]{:S(2)}, u32[]{:S(2)}) async-start(bf16[16,256,256]{2,1,0:T(8,128)(2,1)} %copy-done), calls=%async_computation | async-start | bytes 4194304 | tf_op jit(solution)/shard_map/all_to_all | solution.py:210
  15.5 25.8 %all-to-all-done = bf16[16,256,256]{2,1,0:T(8,128)(2,1)S(1)} async-done(((bf16[16,256,256]{2,1,0:T(8,128)(2,1)}), bf16[16,256,256]{2,1,0:T(8,128)(2,1)S(1)}, u32[]{:S(2)}, u32[]{:S(2)}) %all-to-all-start) | async-done | bytes 2097184 | tf_op jit(solution)/shard_map/all_to_all | solution.py:210
  41.3 3.5 %tiles_other.1 = (bf16[1024,256]{1,0:T(8,128)(2,1)S(1)}, bf16[1024,256]{1,0:T(8,128)(2,1)S(1)}, bf16[256,256]{1,0:T(8,128)(2,1)S(1)}, bf16[256,256]{1,0:T(8,128)...) custom-call(s32[3]{0:T(128)S(1)} %pad_add_fusion.2.refs_0_.here, ...), custom_call_target="tpu_custom_call" | custom-call | flops 536870912 | bytes 6293516 | tf_op jit(solution)/shard_map/tiles_other/pallas_call | solution.py:45
  44.8 3.1 %tiles_own.1 = (bf16[512,256]{1,0:T(8,128)(2,1)S(1)}, bf16[512,256]{1,0:T(8,128)(2,1)S(1)}, bf16[512,256]{1,0:T(8,128)(2,1)S(1)}, bf16[512,256]{1,0:T(8,128)(2,1...) custom-call(s32[3]{0:T(128)S(1)} %pad_add_fusion.2.refs_0_.here, ...), custom_call_target="tpu_custom_call" | custom-call | flops 536870912 | bytes 6293516 | tf_op jit(solution)/shard_map/tiles_own/pallas_call | solution.py:45
  51.5 4.1 %collective-permute-start.6 = (bf16[512,256]{1,0:T(8,128)(2,1)S(1)}, bf16[512,256]{1,0:T(8,128)(2,1)S(1)}, u32[]{:S(2)}, u32[]{:S(2)}) collective-permute-start(bf16[512,256]{1,0:T(8,128)(2,1)S(1)} %get-tuple-element.40), channel_id=1, source_target_pairs={{2,0},{4,2},{6,4},{8,6},{10,8},{12,10},{14,12},{0,14},{3,1},{5,3},... | collective-permute-start | bytes 786440 | tf_op jit(solution)/shard_map/ppermute | solution.py:259
  56.4 2.7 %collective-permute-done.2 = bf16[512,256]{1,0:T(8,128)(2,1)S(1)} collective-permute-done((bf16[512,256]{1,0:T(8,128)(2,1)S(1)}, bf16[512,256]{1,0:T(8,128)(2,1)S(1)}, u32[]{:S(2)}, u32[]{:S(2)}) %collective-permute-start.2) | collective-permute-done | bytes 262176 | tf_op jit(solution)/shard_map/ppermute | solution.py:256
  60.1 3.5 %collective-permute-start.7 = (bf16[512,256]{1,0:T(8,128)(2,1)S(1)}, bf16[512,256]{1,0:T(8,128)(2,1)S(1)}, u32[]{:S(2)}, u32[]{:S(2)}) collective-permute-start(bf16[512,256]{1,0:T(8,128)(2,1)S(1)} %add_convert_fusion.1), channel_id=1, source_target_pairs={{2,0},{4,2},{6,4},{8,6},{10,8},{12,10},{14,12},{0,14},{3,1},{5,3},... | collective-permute-start | bytes 786440 | tf_op jit(solution)/shard_map/ppermute | solution.py:259
  81.1 3.1 %collective-permute-done.14 = bf16[256,256]{1,0:T(8,128)(2,1)S(1)} collective-permute-done((bf16[256,256]{1,0:T(8,128)(2,1)S(1)}, bf16[256,256]{1,0:T(8,128)(2,1)S(1)}, u32[]{:S(2)}, u32[]{:S(2)}) %collective-permute-start.14) | collective-permute-done | bytes 131104 | tf_op jit(solution)/shard_map/ppermute | solution.py:256
  91.3 4.9 %collective-permute-start.19 = (bf16[256,256]{1,0:T(8,128)(2,1)S(1)}, bf16[256,256]{1,0:T(8,128)(2,1)S(1)}, u32[]{:S(2)}, u32[]{:S(2)}) collective-permute-start(bf16[256,256]{1,0:T(8,128)(2,1)S(1)} %add_convert_fusion.5), channel_id=1, source_target_pairs={{0,16},{16,0},{1,17},{17,1},{2,18},{18,2},{3,19},{19,3},{4,20},{20... | collective-permute-start | bytes 393224 | tf_op jit(solution)/shard_map/ppermute | solution.py:253
  97.2 3.1 %node.1 = (bf16[256,512]{1,0:T(8,128)(2,1)}, bf16[256,256]{1,0:T(8,128)(2,1)S(1)}, bf16[256,256]{1,0:T(8,128)(2,1)S(1)}, f32[256,512]{1,0:T(8,128)S(1)}, f32[16,1536]{1,0:T(8,128)S(1)}) custom-call(s32[3]{0:T(128)S(1)} %pad_add_fusion.2.refs_0_.here, bf16[256,512]{1,0:T(8,128)(2,1)S(1)} %copy-done.3, bf16[256,512]{1,0:T(8,128)(2,1)S(1)} %copy-done.7, ...), custom_call_target="tpu_custom_call" | custom-call | bytes 3817484 | tf_op jit(solution)/shard_map/node/pallas_call | solution.py:45
  102.7 2.9 %collective-permute-done.20 = bf16[256,256]{1,0:T(8,128)(2,1)S(1)} collective-permute-done((bf16[256,256]{1,0:T(8,128)(2,1)S(1)}, bf16[256,256]{1,0:T(8,128)(2,1)S(1)}, u32[]{:S(2)}, u32[]{:S(2)}) %collective-permute-start.20) | collective-permute-done | bytes 131104 | tf_op jit(solution)/shard_map/ppermute | solution.py:253
  110.7 3.2 %collective-permute-start.30 = (bf16[256,256]{1,0:T(8,128)(2,1)S(1)}, bf16[256,256]{1,0:T(8,128)(2,1)S(1)}, u32[]{:S(2)}, u32[]{:S(2)}) collective-permute-start(bf16[256,256]{1,0:T(8,128)(2,1)S(1)} %collective-permute-done.28.refs_12_), channel_id=1, source_target_pairs={{0,2},{2,4},{4,6},{6,8},{8,10},{10,12},{12,14},{14,0},{1,3},{3,5},... | collective-permute-start | bytes 393224 | tf_op jit(solution)/shard_map/ppermute | solution.py:256
  115.1 12.1 %collective-permute-start.23 = (bf16[512,256]{1,0:T(8,128)(2,1)S(1)}, bf16[512,256]{1,0:T(8,128)(2,1)S(1)}, u32[]{:S(2)}, u32[]{:S(2)}) collective-permute-start(bf16[512,256]{1,0:T(8,128)(2,1)S(1)} %collective-permute-done.21.refs_5_), channel_id=1, source_target_pairs={{0,2},{2,4},{4,6},{6,8},{8,10},{10,12},{12,14},{14,0},{1,3},{3,5},... | collective-permute-start | bytes 786440 | tf_op jit(solution)/shard_map/ppermute | solution.py:256
  129.9 4.2 %collective-permute-done.33.refs_17_ = bf16[256,256]{1,0:T(8,128)(2,1)S(1)} collective-permute-done((bf16[256,256]{1,0:T(8,128)(2,1)S(1)}, bf16[256,256]{1,0:T(8,128)(2,1)S(1)}, u32[]{:S(2)}, u32[]{:S(2)}) %collective-permute-start.33) | collective-permute-done | bytes 131104 | tf_op jit(solution)/shard_map/ppermute | solution.py:256
  138.2 3.7 %collective-permute-start.31 = (bf16[768,256]{1,0:T(8,128)(2,1)S(1)}, bf16[768,256]{1,0:T(8,128)(2,1)S(1)}, u32[]{:S(2)}, u32[]{:S(2)}) collective-permute-start(bf16[768,256]{1,0:T(8,128)(2,1)S(1)} %pad_maximum_fusion), channel_id=1, source_target_pairs={{0,1},{1,0},{2,3},{3,2},{4,5},{5,4},{6,7},{7,6},{8,9},{9,8},{10,11... | collective-permute-start | bytes 1179656 | tf_op jit(solution)/shard_map/ppermute | solution.py:253
  143.7 5.5 %collective-permute-done.38.refs_22_ = bf16[256,256]{1,0:T(8,128)(2,1)S(1)} collective-permute-done((bf16[256,256]{1,0:T(8,128)(2,1)S(1)}, bf16[256,256]{1,0:T(8,128)(2,1)S(1)}, u32[]{:S(2)}, u32[]{:S(2)}) %collective-permute-start.38) | collective-permute-done | bytes 131104 | tf_op jit(solution)/shard_map/ppermute | solution.py:256
  152.7 3.5 %collective-permute-start.39 = (bf16[256,256]{1,0:T(8,128)(2,1)S(1)}, bf16[256,256]{1,0:T(8,128)(2,1)S(1)}, u32[]{:S(2)}, u32[]{:S(2)}) collective-permute-start(bf16[256,256]{1,0:T(8,128)(2,1)S(1)} %collective-permute-done.38.refs_22_), channel_id=1, source_target_pairs={{0,1},{1,0},{2,3},{3,2},{4,5},{5,4},{6,7},{7,6},{8,9},{9,8},{10,11... | collective-permute-start | bytes 393224 | tf_op jit(solution)/shard_map/ppermute | solution.py:253
  156.2 5.8 %collective-permute-done.39.refs_23_ = bf16[256,256]{1,0:T(8,128)(2,1)S(1)} collective-permute-done((bf16[256,256]{1,0:T(8,128)(2,1)S(1)}, bf16[256,256]{1,0:T(8,128)(2,1)S(1)}, u32[]{:S(2)}, u32[]{:S(2)}) %collective-permute-start.39) | collective-permute-done | bytes 131104 | tf_op jit(solution)/shard_map/ppermute | solution.py:253
  162.0 5.5 %tiles_back.1 = bf16[4096,256]{1,0:T(8,128)(2,1)S(1)} custom-call(s32[3]{0:T(128)S(1)} %pad_add_fusion.2.refs_0_.here, s32[2,256]{1,0:T(2,128)S(1)} %pad_add_fusion.refs_1_, bf16[64,128,128]{2,1,0:T(8,128)(2,1)S(1)} %bitcast.19, bf16[64,128,128]{2,1,0:T(8,128)(2,1)} %collective-permute-done.1.refs_2_.refs_3_, ...), custom_call_target="tpu_custom_call" | custom-call | flops 1073741824 | bytes 10487820 | tf_op jit(solution)/shard_map/tiles_back/pallas_call | solution.py:45
  167.5 37.9 %all_to_all.38.parts = bf16[16,256,256]{2,1,0:T(8,128)(2,1)S(1)} all-to-all(bf16[16,256,256]{2,1,0:T(8,128)(2,1)S(1)} %bitcast.20), channel_id=1, replica_groups=mesh['xly'=8,'co'=2,'z'=8,'xh'=2] {'xly','co'}, dimensions={0} | all-to-all | bytes 4194304 | tf_op jit(solution)/shard_map/all_to_all | solution.py:401
  207.7 13.7 %all_to_all.39 = f32[32,16,128]{2,1,0:T(8,128)S(1)} all-to-all(f32[32,16,128]{2,1,0:T(8,128)S(1)} %bitcast.24), channel_id=1, replica_groups=mesh['xly'=8,'co'=2,'z'=8,'xh'=2] {'xly','co','xh'}, dimensions={0} | all-to-all | bytes 524288 | tf_op jit(solution)/shard_map/all_to_all | solution.py:210
  221.5 15.7 %all_to_all.40 = f32[8,16,128]{2,1,0:T(8,128)S(1)} all-to-all(f32[8,16,128]{2,1,0:T(8,128)S(1)} %broadcast_in_dim.4), channel_id=1, replica_groups=mesh['xly'=8,'co'=2,'z'=8,'xh'=2] {'z'}, dimensions={0} | all-to-all | bytes 131072 | tf_op jit(solution)/shard_map/all_to_all | solution.py:210
  237.2 13.7 %all_to_all.41 = f32[32,16,128]{2,1,0:T(8,128)S(1)} all-to-all(f32[32,16,128]{2,1,0:T(8,128)S(1)} %broadcast_in_dim.5), channel_id=1, replica_groups=mesh['xly'=8,'co'=2,'z'=8,'xh'=2] {'xly','co','xh'}, dimensions={0} | all-to-all | bytes 524288 | tf_op jit(solution)/shard_map/all_to_all | solution.py:210
  (131 shorter events, 62.2 us)
Async XLA Ops:
  0.6 40.7 %collective-permute-start.1 = (bf16[64,128,128]{2,1,0:T(8,128)(2,1)}, bf16[64,128,128]{2,1,0:T(8,128)(2,1)}, u32[]{:S(2)}, u32[]{:S(2)}) collective-permute-start(bf16[64,128,128]{2,1,0:T(8,128)(2,1)} %bitcast.17), channel_id=1, source_target_pairs={{0,16},{16,0},{1,17},{17,1},{2,18},{18,2},{3,19},{19,3},{4,20},{20... | collective-permute-start | bytes 6291464 | tf_op jit(solution)/shard_map/ppermute | solution.py:253
  9.4 31.9 %all-to-all-start = ((bf16[16,256,256]{2,1,0:T(8,128)(2,1)}), bf16[16,256,256]{2,1,0:T(8,128)(2,1)S(1)}, u32[]{:S(2)}, u32[]{:S(2)}) async-start(bf16[16,256,256]{2,1,0:T(8,128)(2,1)} %copy-done), calls=%async_computation | async-start | bytes 4194304 | tf_op jit(solution)/shard_map/all_to_all | solution.py:210
  48.0 11.2 %collective-permute-start.2 = (bf16[512,256]{1,0:T(8,128)(2,1)S(1)}, bf16[512,256]{1,0:T(8,128)(2,1)S(1)}, u32[]{:S(2)}, u32[]{:S(2)}) collective-permute-start(bf16[512,256]{1,0:T(8,128)(2,1)S(1)} %get-tuple-element.36), channel_id=1, source_target_pairs={{0,2},{2,4},{4,6},{6,8},{8,10},{10,12},{12,14},{14,0},{1,3},{3,5},... | collective-permute-start | bytes 786440 | tf_op jit(solution)/shard_map/ppermute | solution.py:256
  50.3 13.8 %collective-permute-start.11 = (bf16[1024,256]{1,0:T(8,128)(2,1)S(1)}, bf16[1024,256]{1,0:T(8,128)(2,1)S(1)}, u32[]{:S(2)}, u32[]{:S(2)}) collective-permute-start(bf16[1024,256]{1,0:T(8,128)(2,1)S(1)} %get-tuple-element.32), channel_id=1, source_target_pairs={{0,1},{1,0},{2,3},{3,2},{4,5},{5,4},{6,7},{7,6},{8,9},{9,8},{10,11... | collective-permute-start | bytes 1572872 | tf_op jit(solution)/shard_map/ppermute | solution.py:253
  51.5 8.5 %collective-permute-start.6 = (bf16[512,256]{1,0:T(8,128)(2,1)S(1)}, bf16[512,256]{1,0:T(8,128)(2,1)S(1)}, u32[]{:S(2)}, u32[]{:S(2)}) collective-permute-start(bf16[512,256]{1,0:T(8,128)(2,1)S(1)} %get-tuple-element.40), channel_id=1, source_target_pairs={{2,0},{4,2},{6,4},{8,6},{10,8},{12,10},{14,12},{0,14},{3,1},{5,3},... | collective-permute-start | bytes 786440 | tf_op jit(solution)/shard_map/ppermute | solution.py:259
  55.6 21.0 %collective-permute-start.10 = (bf16[1024,256]{1,0:T(8,128)(2,1)S(1)}, bf16[1024,256]{1,0:T(8,128)(2,1)S(1)}, u32[]{:S(2)}, u32[]{:S(2)}) collective-permute-start(bf16[1024,256]{1,0:T(8,128)(2,1)S(1)} %get-tuple-element.33), channel_id=1, source_target_pairs={{0,1},{1,0},{2,3},{3,2},{4,5},{5,4},{6,7},{7,6},{8,9},{9,8},{10,11... | collective-permute-start | bytes 1572872 | tf_op jit(solution)/shard_map/ppermute | solution.py:253
  59.2 8.5 %collective-permute-start.3 = (bf16[512,256]{1,0:T(8,128)(2,1)S(1)}, bf16[512,256]{1,0:T(8,128)(2,1)S(1)}, u32[]{:S(2)}, u32[]{:S(2)}) collective-permute-start(bf16[512,256]{1,0:T(8,128)(2,1)S(1)} %add_convert_fusion.4), channel_id=1, source_target_pairs={{0,2},{2,4},{4,6},{6,8},{8,10},{10,12},{12,14},{14,0},{1,3},{3,5},... | collective-permute-start | bytes 786440 | tf_op jit(solution)/shard_map/ppermute | solution.py:256
  60.1 13.1 %collective-permute-start.7 = (bf16[512,256]{1,0:T(8,128)(2,1)S(1)}, bf16[512,256]{1,0:T(8,128)(2,1)S(1)}, u32[]{:S(2)}, u32[]{:S(2)}) collective-permute-start(bf16[512,256]{1,0:T(8,128)(2,1)S(1)} %add_convert_fusion.1), channel_id=1, source_target_pairs={{2,0},{4,2},{6,4},{8,6},{10,8},{12,10},{14,12},{0,14},{3,1},{5,3},... | collective-permute-start | bytes 786440 | tf_op jit(solution)/shard_map/ppermute | solution.py:259
  67.8 11.4 %collective-permute-start.4 = (bf16[512,256]{1,0:T(8,128)(2,1)S(1)}, bf16[512,256]{1,0:T(8,128)(2,1)S(1)}, u32[]{:S(2)}, u32[]{:S(2)}) collective-permute-start(bf16[512,256]{1,0:T(8,128)(2,1)S(1)} %add_convert_fusion.3), channel_id=1, source_target_pairs={{0,2},{2,4},{4,6},{6,8},{8,10},{10,12},{12,14},{14,0},{1,3},{3,5},... | collective-permute-start | bytes 786440 | tf_op jit(solution)/shard_map/ppermute | solution.py:256
  73.3 13.8 %collective-permute-start.8 = (bf16[512,256]{1,0:T(8,128)(2,1)S(1)}, bf16[512,256]{1,0:T(8,128)(2,1)S(1)}, u32[]{:S(2)}, u32[]{:S(2)}) collective-permute-start(bf16[512,256]{1,0:T(8,128)(2,1)S(1)} %add_convert_fusion), channel_id=1, source_target_pairs={{2,0},{4,2},{6,4},{8,6},{10,8},{12,10},{14,12},{0,14},{3,1},{5,3},... | collective-permute-start | bytes 786440 | tf_op jit(solution)/shard_map/ppermute | solution.py:259
  79.3 8.7 %collective-permute-start.5 = (bf16[512,256]{1,0:T(8,128)(2,1)S(1)}, bf16[512,256]{1,0:T(8,128)(2,1)S(1)}, u32[]{:S(2)}, u32[]{:S(2)}) collective-permute-start(bf16[512,256]{1,0:T(8,128)(2,1)S(1)} %add_convert_fusion.2), channel_id=1, source_target_pairs={{0,2},{2,4},{4,6},{6,8},{8,10},{10,12},{12,14},{14,0},{1,3},{3,5},... | collective-permute-start | bytes 786440 | tf_op jit(solution)/shard_map/ppermute | solution.py:256
  105.6 9.5 %collective-permute-start.21 = (bf16[512,256]{1,0:T(8,128)(2,1)S(1)}, bf16[512,256]{1,0:T(8,128)(2,1)S(1)}, u32[]{:S(2)}, u32[]{:S(2)}) collective-permute-start(bf16[512,256]{1,0:T(8,128)(2,1)S(1)} %constant_dynamic-update-slice_fusion.refs_4_), channel_id=1, source_target_pairs={{0,2},{2,4},{4,6},{6,8},{8,10},{10,12},{12,14},{14,0},{1,3},{3,5},... | collective-permute-start | bytes 786440 | tf_op jit(solution)/shard_map/ppermute | solution.py:256
  110.7 16.4 %collective-permute-start.30 = (bf16[256,256]{1,0:T(8,128)(2,1)S(1)}, bf16[256,256]{1,0:T(8,128)(2,1)S(1)}, u32[]{:S(2)}, u32[]{:S(2)}) collective-permute-start(bf16[256,256]{1,0:T(8,128)(2,1)S(1)} %collective-permute-done.28.refs_12_), channel_id=1, source_target_pairs={{0,2},{2,4},{4,6},{6,8},{8,10},{10,12},{12,14},{14,0},{1,3},{3,5},... | collective-permute-start | bytes 393224 | tf_op jit(solution)/shard_map/ppermute | solution.py:256
  113.9 15.5 %collective-permute-start.29 = (bf16[256,256]{1,0:T(8,128)(2,1)S(1)}, bf16[256,256]{1,0:T(8,128)(2,1)S(1)}, u32[]{:S(2)}, u32[]{:S(2)}) collective-permute-start(bf16[256,256]{1,0:T(8,128)(2,1)S(1)} %collective-permute-done.28.refs_12_), channel_id=1, source_target_pairs={{2,0},{4,2},{6,4},{8,6},{10,8},{12,10},{14,12},{0,14},{3,1},{5,3},... | collective-permute-start | bytes 393224 | tf_op jit(solution)/shard_map/ppermute | solution.py:259
  113.9 22.8 %collective-permute-start.22 = (bf16[512,256]{1,0:T(8,128)(2,1)S(1)}, bf16[512,256]{1,0:T(8,128)(2,1)S(1)}, u32[]{:S(2)}, u32[]{:S(2)}) collective-permute-start(bf16[512,256]{1,0:T(8,128)(2,1)S(1)} %constant_dynamic-update-slice_fusion.refs_4_), channel_id=1, source_target_pairs={{2,0},{4,2},{6,4},{8,6},{10,8},{12,10},{14,12},{0,14},{3,1},{5,3},... | collective-permute-start | bytes 786440 | tf_op jit(solution)/shard_map/ppermute | solution.py:259
  115.1 22.9 %collective-permute-start.23 = (bf16[512,256]{1,0:T(8,128)(2,1)S(1)}, bf16[512,256]{1,0:T(8,128)(2,1)S(1)}, u32[]{:S(2)}, u32[]{:S(2)}) collective-permute-start(bf16[512,256]{1,0:T(8,128)(2,1)S(1)} %collective-permute-done.21.refs_5_), channel_id=1, source_target_pairs={{0,2},{2,4},{4,6},{6,8},{8,10},{10,12},{12,14},{14,0},{1,3},{3,5},... | collective-permute-start | bytes 786440 | tf_op jit(solution)/shard_map/ppermute | solution.py:256
  136.7 14.5 %collective-permute-start.24 = (bf16[512,256]{1,0:T(8,128)(2,1)S(1)}, bf16[512,256]{1,0:T(8,128)(2,1)S(1)}, u32[]{:S(2)}, u32[]{:S(2)}) collective-permute-start(bf16[512,256]{1,0:T(8,128)(2,1)S(1)} %collective-permute-done.22.refs_6_), channel_id=1, source_target_pairs={{2,0},{4,2},{6,4},{8,6},{10,8},{12,10},{14,12},{0,14},{3,1},{5,3},... | collective-permute-start | bytes 786440 | tf_op jit(solution)/shard_map/ppermute | solution.py:259
  137.9 13.7 %collective-permute-start.25 = (bf16[512,256]{1,0:T(8,128)(2,1)S(1)}, bf16[512,256]{1,0:T(8,128)(2,1)S(1)}, u32[]{:S(2)}, u32[]{:S(2)}) collective-permute-start(bf16[512,256]{1,0:T(8,128)(2,1)S(1)} %collective-permute-done.23.refs_7_), channel_id=1, source_target_pairs={{0,2},{2,4},{4,6},{6,8},{8,10},{10,12},{12,14},{14,0},{1,3},{3,5},... | collective-permute-start | bytes 786440 | tf_op jit(solution)/shard_map/ppermute | solution.py:256
  138.2 17.9 %collective-permute-start.31 = (bf16[768,256]{1,0:T(8,128)(2,1)S(1)}, bf16[768,256]{1,0:T(8,128)(2,1)S(1)}, u32[]{:S(2)}, u32[]{:S(2)}) collective-permute-start(bf16[768,256]{1,0:T(8,128)(2,1)S(1)} %pad_maximum_fusion), channel_id=1, source_target_pairs={{0,1},{1,0},{2,3},{3,2},{4,5},{5,4},{6,7},{7,6},{8,9},{9,8},{10,11... | collective-permute-start | bytes 1179656 | tf_op jit(solution)/shard_map/ppermute | solution.py:253
  143.1 9.7 %collective-permute-start.34 = (bf16[512,256]{1,0:T(8,128)(2,1)S(1)}, bf16[512,256]{1,0:T(8,128)(2,1)S(1)}, u32[]{:S(2)}, u32[]{:S(2)}) collective-permute-start(bf16[512,256]{1,0:T(8,128)(2,1)S(1)} %pad_maximum_fusion.1), channel_id=1, source_target_pairs={{0,1},{1,0},{2,3},{3,2},{4,5},{5,4},{6,7},{7,6},{8,9},{9,8},{10,11... | collective-permute-start | bytes 786440 | tf_op jit(solution)/shard_map/ppermute | solution.py:253
  149.3 12.7 %collective-permute-start.37 = (bf16[512,256]{1,0:T(8,128)(2,1)S(1)}, bf16[512,256]{1,0:T(8,128)(2,1)S(1)}, u32[]{:S(2)}, u32[]{:S(2)}) collective-permute-start(bf16[512,256]{1,0:T(8,128)(2,1)S(1)} %pad_maximum_fusion.2), channel_id=1, source_target_pairs={{0,1},{1,0},{2,3},{3,2},{4,5},{5,4},{6,7},{7,6},{8,9},{9,8},{10,11... | collective-permute-start | bytes 786440 | tf_op jit(solution)/shard_map/ppermute | solution.py:253
  151.3 10.7 %collective-permute-start.26 = (bf16[512,256]{1,0:T(8,128)(2,1)S(1)}, bf16[512,256]{1,0:T(8,128)(2,1)S(1)}, u32[]{:S(2)}, u32[]{:S(2)}) collective-permute-start(bf16[512,256]{1,0:T(8,128)(2,1)S(1)} %collective-permute-done.24.refs_8_), channel_id=1, source_target_pairs={{2,0},{4,2},{6,4},{8,6},{10,8},{12,10},{14,12},{0,14},{3,1},{5,3},... | collective-permute-start | bytes 786440 | tf_op jit(solution)/shard_map/ppermute | solution.py:259
  151.7 10.3 %collective-permute-start.27 = (bf16[512,256]{1,0:T(8,128)(2,1)S(1)}, bf16[512,256]{1,0:T(8,128)(2,1)S(1)}, u32[]{:S(2)}, u32[]{:S(2)}) collective-permute-start(bf16[512,256]{1,0:T(8,128)(2,1)S(1)} %collective-permute-done.25.refs_9_), channel_id=1, source_target_pairs={{0,2},{2,4},{4,6},{6,8},{8,10},{10,12},{12,14},{14,0},{1,3},{3,5},... | collective-permute-start | bytes 786440 | tf_op jit(solution)/shard_map/ppermute | solution.py:256
  152.7 9.2 %collective-permute-start.39 = (bf16[256,256]{1,0:T(8,128)(2,1)S(1)}, bf16[256,256]{1,0:T(8,128)(2,1)S(1)}, u32[]{:S(2)}, u32[]{:S(2)}) collective-permute-start(bf16[256,256]{1,0:T(8,128)(2,1)S(1)} %collective-permute-done.38.refs_22_), channel_id=1, source_target_pairs={{0,1},{1,0},{2,3},{3,2},{4,5},{5,4},{6,7},{7,6},{8,9},{9,8},{10,11... | collective-permute-start | bytes 393224 | tf_op jit(solution)/shard_map/ppermute | solution.py:253
  (32 other events, 350.1 us)

commit v3 on v2

v3 whole, which is shorter than its diff:
```python
import math

import jax
import jax.numpy as jnp
from jax import lax
from jax.experimental import pallas as pl
from jax.experimental.pallas import tpu as pltpu
from jax.sharding import Mesh, PartitionSpec as P

BF, F32 = jnp.bfloat16, jnp.float32
UNROLL = 16
PARTS = 2
MIB = 1 << 20
ALL = ("xly", "co", "z", "xh")
ROW, COL = ("xly", "co"), ("z", "xh")
NEAR = ("xly", "co", "xh")
SHARED = ((0, 0), (1, 0), (0, 1), (1, 1))


def dot(left, right):
    return jnp.dot(left, right, preferred_element_type=F32)


def across(left, right):
    return lax.dot_general(left, right, (((0,), (0,)), ((), ())), preferred_element_type=F32)


def times_transposed(left, right):
    return lax.dot_general(left, right, (((1,), (1,)), ((), ())), preferred_element_type=F32)


def sigmoid(values):
    return 1.0 / (1.0 + jnp.exp(-values))


def silu_slope(values):
    sigma = sigmoid(values)
    return sigma * (1.0 + values * (1.0 - sigma))


def call(kernel, out_shape, *args, scratch=(), smem=0, vmem=40, flops=0, name=None, far=()):
    def place(i):
        return pl.BlockSpec(memory_space=pltpu.HBM if i in far else pltpu.VMEM)

    moved = sum(a.size * a.dtype.itemsize for a in args)
    moved += sum(math.prod(s.shape) * s.dtype.itemsize for s in jax.tree.leaves(out_shape))
    return pl.pallas_call(
        kernel,
        out_shape=out_shape,
        in_specs=[pl.BlockSpec(memory_space=pltpu.SMEM)] * smem
        + [place(i) for i in range(smem, len(args))],
        out_specs=(pl.BlockSpec(memory_space=pltpu.VMEM),) * len(out_shape),
        scratch_shapes=list(scratch),
        compiler_params=pltpu.CompilerParams(vmem_limit_bytes=vmem * MIB),
        cost_estimate=pl.CostEstimate(flops=flops, bytes_accessed=moved, transcendentals=0),
        name=name,
    )(*args)


def add(*terms):
    total = terms[0].astype(F32)
    for term in terms[1:]:
        total = total + term.astype(F32)
    return total


def message_kernel(feats, base, down_t, up, pieces):
    low = times_transposed(feats[...], down_t[...]).astype(BF)
    pre = dot(feats[...], base[...]) + dot(low, up[...])
    message = (pre * sigmoid(pre)).astype(BF)
    width = pieces.shape[2]
    for i in range(pieces.shape[0]):
        pieces[i] = message[:, i % 2 * width : (i % 2 + 1) * width]


def clear(total):
    rows = total.shape[0] - 128

    def step(i, carry):
        at = pl.ds(pl.multiple_of(i * 256, 256), 256)
        total[at, :] = jnp.zeros((256, total.shape[1]), F32)
        return carry

    lax.fori_loop(0, rows // 256, step, 0)


def fetch_tiles(meta, stacks, near, sems):
    slots = near.shape[1]
    size = slots // PARTS
    copies = []
    for owner, stack in enumerate(stacks):
        for part in range(PARTS):
            at = pl.ds(part * size, size)
            source = stack[0].at[at] if len(stack) == 1 else stack[part]
            live = meta[owner, 2 * slots] > part * size
            copy = pltpu.make_async_copy(
                source, near.at[owner, at], sems.at[owner * PARTS + part]
            )
            pl.when(live)(copy.start)
            copies.append((live, copy))
    return copies


def add_tiles(meta, owner, weights, copies, source, total, row_at, col_at, backward):
    slots = weights.shape[0]
    spare = total.shape[0] - 128
    count = meta[owner, 2 * slots]
    size = slots // PARTS

    def group(i, carry):
        products, places = [], []
        for j in range(UNROLL):
            slot = i * UNROLL + j
            live = slot < count
            row = row_at(jnp.where(live, meta[owner, 2 * slot], 0))
            col = col_at(jnp.where(live, meta[owner, 2 * slot + 1], 0))
            begin, end = (row, col) if backward else (col, row)
            places.append(pl.multiple_of(jnp.where(live, end, spare), 128))
            block = source[pl.ds(pl.multiple_of(begin, 128), 128), :]
            tile = weights[slot]
            products.append(across(tile, block) if backward else dot(tile, block))
        for product, at in zip(products, places):
            total[pl.ds(at, 128), :] += product
        return carry

    for part, (wanted, copy) in enumerate(copies):
        pl.when(wanted)(copy.wait)
        end = jnp.minimum(count, (part + 1) * size)
        lax.fori_loop(part * size // UNROLL, (end + UNROLL - 1) // UNROLL, group, 0)


def forward_kernel(groups, n_z, here, meta, w0, w1, source, *rest):
    outs, (total, near, sems) = rest[:-3], rest[-3:]
    copies = fetch_tiles(meta, [[w0], [w1]], near, sems)
    z, xh = here[1], here[2]
    nodes = (total.shape[0] - 128) // (4 * n_z)
    clear(total)
    for owner in range(2):

        def row_at(tile, owner=owner):
            return owner * (2 * n_z * nodes) + tile * 128

        def col_at(tile):
            return tile * 128

        parts = copies[owner * PARTS : (owner + 1) * PARTS]
        add_tiles(meta, owner, near.at[owner], parts, source, total, row_at, col_at, False)
    for out, places in zip(outs, groups):
        for k, (owner, distance, side) in enumerate(places):
            to = lax.rem(z + (distance + n_z), n_z) * 2 + (xh ^ side)
            at = pl.multiple_of((owner * 2 * n_z + to) * nodes, nodes)
            out[k * nodes : (k + 1) * nodes] = total[pl.ds(at, nodes), :].astype(BF)


def backward_kernel(distances, n_z, here, meta, w0, w1, w2, w3, w4, w5, *rest):
    shards, (out, total, source, near, sems) = rest[:-5], rest[-5:]
    copies = fetch_tiles(meta, [[w0], [w1], [w2, w3], [w4, w5]], near, sems)
    z, xh = here[1], here[2]
    block = source.shape[0] // n_z
    nodes = block // 4
    for shard, distance in zip(shards, distances):
        at = lax.rem(z + (distance + n_z), n_z) * block
        source[pl.ds(pl.multiple_of(at, block), block), :] = shard[...]
    clear(total)
    for owner, (core, side) in enumerate(SHARED):

        def row_at(tile, core=core):
            place = core * 2 + (((tile >> 1) & 1) ^ xh)
            return (tile >> 2) * block + place * nodes + (tile & 1) * 128

        def col_at(tile, side=side):
            return ((tile >> 1) * 2 + (xh ^ side)) * nodes + (tile & 1) * 128

        parts = copies[owner * PARTS : (owner + 1) * PARTS]
        add_tiles(meta, owner, near.at[owner], parts, source, total, row_at, col_at, True)

    def finish(i, carry):
        at = pl.ds(pl.multiple_of(i * 256, 256), 256)
        out[at, :] = total[at, :].astype(BF)
        return carry

    lax.fori_loop(0, out.shape[0] // 256, finish, 0)


def node_kernel(here, feats, cot, t0, t1, t2, t3, other, base, down_t, up, new_out, keep, give, partial_out, grads):
    first = here[0] == 0
    full = feats.shape[1]
    half = full // 2
    nodes = feats.shape[0]
    mine = add(t0[:nodes], t1[:nodes], t2[:nodes], t3[...]).astype(BF)
    rest = other[...]
    agg = [jnp.where(first, mine, rest), jnp.where(first, rest, mine)]
    joined = jnp.concatenate([feats[...]] + agg, axis=1)
    low = times_transposed(joined, down_t[...]).astype(BF)
    pre = dot(joined, base[...]) + dot(low, up[...])
    sigma = sigmoid(pre)
    cot_wide = cot[...].astype(F32)
    slope = (cot_wide * (sigma * (1.0 + pre * (1.0 - sigma)))).astype(BF)
    mix = times_transposed(slope, up[...]).astype(BF)
    joined_grad = times_transposed(slope, base[...]) + dot(mix, down_t[...])
    agg_grad = joined_grad[:, full:].astype(BF)
    width = half // 2
    left = here[2] == 0
    for out, values in (
        (keep, jnp.where(first, agg_grad[:, :half], agg_grad[:, half:])),
        (give, jnp.where(first, agg_grad[:, half:], agg_grad[:, :half])),
    ):
        out[:nodes] = jnp.where(left, values[:, :width], values[:, width:])
        out[nodes:] = jnp.where(left, values[:, width:], values[:, :width])
    new_out[...] = (feats[...].astype(F32) + pre * sigma).astype(BF)
    partial_out[...] = cot_wide + joined_grad[:, :full]
    grads[:, : 2 * full] = across(mix, joined)
    grads[:, 2 * full :] = across(low, slope)


def edge_kernel(feats, parts, partial, base, down_t, up, feat_out, grads):
    full = feats.shape[1]
    low = times_transposed(feats[...], down_t[...]).astype(BF)
    pre = dot(feats[...], base[...]) + dot(low, up[...])
    factor = silu_slope(pre)
    quarters = [None] * 4
    for i in range(parts.shape[0]):
        term = parts[i].astype(F32)
        quarters[i % 4] = term if quarters[i % 4] is None else quarters[i % 4] + term
    slope = (jnp.concatenate(quarters, axis=1) * factor).astype(BF)
    mix = times_transposed(slope, up[...]).astype(BF)
    grads[:, :full] = across(mix, feats[...])
    grads[:, full:] = across(low, slope)
    feat_out[...] = (
        partial[...] + times_transposed(slope, base[...]) + dot(mix, down_t[...])
    ).astype(BF)


def exchange(pieces, axes):
    shape = pieces.shape
    flat = pieces.reshape(shape[0] * shape[1], shape[2])
    return lax.all_to_all(flat, axes, split_axis=0, concat_axis=0, tiled=True)


def sum_over_all(grads):
    n_near, n_z = lax.axis_size(NEAR), lax.axis_size("z")
    rank, wide = grads.shape
    lines = -(-rank * wide // (n_near * 2048)) * 16
    grads = jnp.pad(grads.astype(BF).reshape(-1), (0, n_near * lines * 128 - rank * wide))
    mine = exchange(grads.reshape(n_near, lines, 128), NEAR)
    mine = mine.reshape(n_near, lines, 128).astype(F32).sum(axis=0).astype(BF)
    spread = jnp.broadcast_to(mine[None], (n_z, lines, 128))
    mine = exchange(spread, "z").reshape(n_z, lines, 128).astype(F32).sum(axis=0).astype(BF)
    spread = jnp.broadcast_to(mine[None], (n_near, lines, 128))
    whole = exchange(spread, NEAR).astype(F32).reshape(-1)
    return whole[: rank * wide].reshape(rank, wide)


def body(
    node_feats,
    cotangent,
    edge_base,
    edge_down,
    edge_up,
    node_base,
    node_down,
    node_up,
    tile_weight,
    tile_place,
    tile_count,
):
    nodes, full = node_feats.shape
    n_row = lax.axis_size(ROW)
    n_col = lax.axis_size(COL)
    n_z = lax.axis_size("z")
    n_up, n_down = n_z // 2, (n_z - 1) // 2
    rank = edge_up.shape[0]
    half, width = full // 2, full // 4
    tiles = tile_weight[0, 0]
    slots = tiles.shape[0]
    sds = jax.ShapeDtypeStruct

    def swap(values, axis):
        return lax.ppermute(values, axis, [(0, 1), (1, 0)])

    def up(values):
        return lax.ppermute(values, "z", [(i, (i + 1) % n_z) for i in range(n_z)])

    def down(values):
        return lax.ppermute(values, "z", [((i + 1) % n_z, i) for i in range(n_z)])

    meta = jnp.concatenate([tile_place.reshape(1, 2 * slots), tile_count.reshape(1, 1)], axis=1)
    meta = jnp.pad(meta, ((0, 0), (0, 256 - meta.shape[1])))
    meta = jnp.concatenate([meta, swap(meta, "co")], axis=0)
    tiles_c = swap(tiles, "co")
    meta = jnp.concatenate([meta, swap(meta, "xh")], axis=0)
    here = jnp.stack([lax.axis_index("co"), lax.axis_index("z"), lax.axis_index("xh")])
    here = here.astype(jnp.int32)

    pieces = call(
        message_kernel,
        (sds((n_row, nodes, half), BF),),
        node_feats,
        edge_base,
        edge_down.T,
        edge_up,
        name="message",
    )[0]
    source = exchange(pieces, ROW)

    flat = [d for i in range(n_up) for d in (n_up - i, i - n_down)]
    mirror = {d: d if d == n_up else -d for d in flat}
    first, second = flat[: n_z // 2], flat[n_z // 2 :]
    groups = [[(1, mirror[d], 1) for d in part] for part in (first, second)]
    groups += [[(0, d, 0), (0, d, 1)] for d in flat] + [[(1, mirror[d], 0)] for d in flat]

    def forward(*refs):
        forward_kernel(groups, n_z, *refs)

    outs = call(
        forward,
        tuple(sds((len(places) * nodes, half), BF) for places in groups),
        here,
        meta,
        tiles,
        tiles_c,
        source,
        scratch=[
            pltpu.VMEM((2 * n_col * nodes + 128, half), F32),
            pltpu.VMEM((2, slots, 128, 128), BF),
            pltpu.SemaphoreType.DMA((2 * PARTS,)),
        ],
        smem=2,
        far=(2, 3),
        flops=4 * slots * 128 * 128 * half,
        name="tiles",
    )
    sent, own, kept = outs[:2], dict(zip(flat, outs[2 : 2 + n_z])), outs[2 + n_z :]
    got = [swap(block, "xh") for block in sent]
    tiles_near, got[0] = lax.optimization_barrier((tiles[: slots // 2], got[0]))
    tiles_x = [swap(tiles_near, "xh")]
    other = {}
    for i, d in enumerate(flat):
        k = i % len(first)
        other[d] = add(kept[i], got[i // len(first)][k * nodes : (k + 1) * nodes]).astype(BF)

    def ring_sum(blocks, up, down):
        rising = up(blocks[n_up])
        falling = down(blocks[-n_down]) if n_down else jnp.zeros_like(rising)
        for k in range(1, n_up):
            rising = up(add(rising, blocks[n_up - k]).astype(BF))
            if k < n_down:
                falling = down(add(falling, blocks[k - n_down]).astype(BF))
        return [blocks[0], rising, falling]

    terms = ring_sum(own, up, down)
    agg_other = add(*ring_sum(other, down, up)).astype(BF)
    agg_other, tiles_x[0] = lax.optimization_barrier((agg_other, tiles_x[0]))
    agg_other = swap(agg_other, "co")
    across_x = swap(add(*[term[nodes:] for term in terms]).astype(BF), "xh")
    new_feats, keep, give, partial_grad, node_grads = call(
        node_kernel,
        (
            sds((nodes, full), BF),
            sds((2 * nodes, width), BF),
            sds((2 * nodes, width), BF),
            sds((nodes, full), F32),
            sds((rank, 3 * full), F32),
        ),
        here,
        node_feats,
        cotangent,
        *terms,
        across_x,
        agg_other,
        node_base,
        node_down.T,
        node_up,
        smem=1,
        name="node",
    )

    tiles_cx = [swap(lax.optimization_barrier((tiles_x[0], keep))[0], "co")]
    both = jnp.stack([keep, swap(give, "co")]).reshape(2, 2, nodes, width)
    beyond = swap(both[:, 1].reshape(2 * nodes, width), "xh")
    tiles_near, beyond = lax.optimization_barrier((tiles[slots // 2 :], beyond))
    tiles_x.append(swap(tiles_near, "xh"))
    beyond = beyond.reshape(2, nodes, width)
    shards = {0: jnp.stack([both[:, 0], beyond], axis=1).reshape(4 * nodes, width)}
    for k in range(1, n_up + 1):
        shards[-k] = up(shards[1 - k])
        if k <= n_down:
            shards[k] = down(shards[k - 1])

    late = [1 - n_up, n_down] if n_down else [0]
    tiles_x[1] = lax.optimization_barrier([tiles_x[1]] + [shards[d] for d in late])[0]
    tiles_cx.append(swap(tiles_x[1], "co"))

    def backward(*refs):
        backward_kernel(list(shards), n_z, *refs)

    rows = 2 * n_row * nodes
    partial_cols = call(
        backward,
        (sds((rows, width), BF),),
        here,
        meta,
        tiles,
        tiles_c,
        *tiles_x,
        *tiles_cx,
        *shards.values(),
        scratch=[
            pltpu.VMEM((rows + 128, width), F32),
            pltpu.VMEM((2 * n_col * nodes, width), BF),
            pltpu.VMEM((4, slots, 128, 128), BF),
            pltpu.SemaphoreType.DMA((4 * PARTS,)),
        ],
        smem=2,
        far=(2, 3, 4, 5, 6, 7),
        flops=8 * slots * 128 * 128 * width,
        name="tiles_back",
    )[0]
    parts = exchange(partial_cols.reshape(2 * n_row, nodes, width), NEAR)
    feat_grad, edge_grads = call(
        edge_kernel,
        (sds((nodes, full), BF), sds((rank, 2 * full), F32)),
        node_feats,
        parts.reshape(2 * n_row, nodes, width),
        partial_grad,
        edge_base,
        edge_down.T,
        edge_up,
        name="edge",
    )
    grads = sum_over_all(jnp.concatenate([edge_grads, node_grads], axis=1))
    grads = grads * (1.0 / math.sqrt(nodes * n_row * n_col))
    return (
        new_feats,
        feat_grad,
        grads[:, :full].T,
        grads[:, full : 2 * full],
        grads[:, 2 * full : 4 * full].T,
        grads[:, 4 * full :],
    )


def solution(mesh):
    n_row, n_col = mesh.shape["row"], mesh.shape["col"]
    fine = Mesh(mesh.devices.reshape(n_row // 2, 2, n_col // 2, 2), ALL)
    nodes = P(ROW + COL, None)
    placed = (
        nodes,
        nodes,
        P(),
        P(),
        P(),
        P(),
        P(),
        P(),
        P(ROW, COL, None, None, None),
        P(ROW, COL, None, None),
        P(ROW, COL),
    )
    return jax.shard_map(
        body,
        mesh=fine,
        in_specs=placed,
        out_specs=(nodes, nodes, P(), P(), P(), P()),
        check_vma=False,
    )
```

time: 257 us -> 239 us (0.930); the launches traced: 252 us -> 238 us
  blocking collectives: 81 us -> 36.5 us
  waiting for transfers between devices: 61.7 us -> 99.5 us
  starting transfers between devices: 82.4 us -> 72.2 us
    all_to_all x1 -> x0, blocking collectives: 37.9 us -> none  [body(): lax.all_to_all(partial_cols, ROW, split_axis=0, concat_axis=0, tiled=True)]
    ppermute x16 -> x11, starting transfers between devices: 31.8 us -> 2.45 us  [up(): return lax.ppermute(values, 'z', [(i, (i + 1) % n_z) for i in range(n_z)])]
    ppermute x12 -> x13, waiting for transfers between devices: 12.1 us -> 36.6 us  [swap(): return lax.ppermute(values, axis, [(0, 1), (1, 0)])]
    ppermute x12 -> x10, waiting for transfers between devices: 1.59 us -> 11.7 us  [down(): return lax.ppermute(values, 'z', [((i + 1) % n_z, i) for i in range(n_z)])]
    ppermute x12 -> x13, starting transfers between devices: 26.9 us -> 36 us  [swap(): return lax.ppermute(values, axis, [(0, 1), (1, 0)])]
    all_to_all x1 -> x2, starting transfers between devices: 3.92 us -> 11.7 us  [exchange(): return lax.all_to_all(flat, axes, split_axis=0, concat_axis=0, tiled=True)]
    all_to_all x3, blocking collectives: 43.1 us -> 36.5 us  [exchange(): return lax.all_to_all(flat, axes, split_axis=0, concat_axis=0, tiled=True)]
    all_to_all x1 -> x2, waiting for transfers between devices: 25.8 us -> 28.7 us  [exchange(): return lax.all_to_all(flat, axes, split_axis=0, concat_axis=0, tiled=True)]
  transfers between devices with their start and end apart: 41 -> 36, of which waited for: 17 -> 21; matrix products, arithmetic and copies ran while one was open for 0% -> 1% of each run, Pallas kernels for 0% -> 0%
where the time goes in v3:
time: 239 us; the launch traced here: 238 us
  waiting for transfers between devices  99.5 us (42%)
  starting transfers between devices  72.2 us (30%)
  blocking collectives  36.5 us (15%)
  Pallas kernels  18.3 us (8%)
  local copies, waits for them, and re-layouts  8.05 us (3%)
    ppermute x13, waiting for transfers between devices, swap(): return lax.ppermute(values, axis, [(0, 1), (1, 0)])  36.6 us
    all_to_all x3, blocking collectives, exchange(): return lax.all_to_all(flat, axes, split_axis=0, concat_axis=0, tiled=True)  36.5 us
    ppermute x13, starting transfers between devices, swap(): return lax.ppermute(values, axis, [(0, 1), (1, 0)])  36 us
    all_to_all x2, waiting for transfers between devices, exchange(): return lax.all_to_all(flat, axes, split_axis=0, concat_axis=0, tiled=True)  28.7 us
    ppermute x11, waiting for transfers between devices, up(): return lax.ppermute(values, 'z', [(i, (i + 1) % n_z) for i in range(n_z)])  22.6 us
    ppermute x10, starting transfers between devices, down(): return lax.ppermute(values, 'z', [((i + 1) % n_z, i) for i in range(n_z)])  22.1 us
    pallas_call x5, Pallas kernels, call(): pl.pallas_call(kernel, out_shape=out_shape, in_specs=[pl.BlockSpec(memory...  18.3 us
    all_to_all x2, starting transfers between devices, exchange(): return lax.all_to_all(flat, axes, split_axis=0, concat_axis=0, tiled=True)  11.7 us
  transfers between devices with their start and end apart: 36, of which 21 were waited for; matrix products, arithmetic and copies ran while one was open for 1% of the time, Pallas kernels for 0%

profile of v3, /device:TPU:1, one launch (start us, length us, event | category | flops | bytes accessed | tf_op | source)
XLA Modules:
  0.0 237.8 jit_solution(18083646590809026170)
XLA Ops:
  0.6 3.3 %collective-permute-start.2 = (bf16[64,128,128]{2,1,0:T(8,128)(2,1)}, bf16[64,128,128]{2,1,0:T(8,128)(2,1)}, u32[]{:S(2)}, u32[]{:S(2)}) collective-permute-start(bf16[64,128,128]{2,1,0:T(8,128)(2,1)} %bitcast.24), channel_id=1, source_target_pairs={{0,16},{16,0},{1,17},{17,1},{2,18},{18,2},{3,19},{19,3},{4,20},{20... | collective-permute-start | bytes 6291464 | tf_op jit(solution)/shard_map/ppermute | solution.py:279
  9.4 4.5 %all-to-all-start = ((bf16[16,256,256]{2,1,0:T(8,128)(2,1)}), bf16[16,256,256]{2,1,0:T(8,128)(2,1)}, u32[]{:S(2)}, u32[]{:S(2)}) async-start(bf16[16,256,256]{2,1,0:T(8,128)(2,1)} %copy-done.1), calls=%async_computation | async-start | bytes 4194304 | tf_op jit(solution)/shard_map/all_to_all | solution.py:237
  18.0 22.9 %collective-permute-done.1 = s32[2,256]{1,0:T(2,128)S(1)} collective-permute-done((s32[2,256]{1,0:T(2,128)S(1)}, s32[2,256]{1,0:T(2,128)S(1)}, u32[]{:S(2)}, u32[]{:S(2)}) %collective-permute-start.1) | collective-permute-done | bytes 2080 | tf_op jit(solution)/shard_map/ppermute | solution.py:279
  41.9 5.5 %tiles.1 = (bf16[1024,256]{1,0:T(8,128)(2,1)S(1)}, bf16[1024,256]{1,0:T(8,128)(2,1)S(1)}, bf16[512,256]{1,0:T(8,128)(2,1)S(1)}, bf16[512,256]{1,0:T(8,128)(2,1)S...) custom-call(s32[3]{0:T(128)S(1)} %pad_add_fusion.3.refs_0_.here, ...), custom_call_target="tpu_custom_call" | custom-call | flops 1073741824 | bytes 10489868 | tf_op jit(solution)/shard_map/tiles/pallas_call | solution.py:47
  61.0 5.1 %collective-permute-done.12 = bf16[1024,256]{1,0:T(8,128)(2,1)S(1)} collective-permute-done((bf16[1024,256]{1,0:T(8,128)(2,1)S(1)}, bf16[1024,256]{1,0:T(8,128)(2,1)S(1)}, u32[]{:S(2)}, u32[]{:S(2)}) %collective-permute-start.12) | collective-permute-done | bytes 524320 | tf_op jit(solution)/shard_map/ppermute | solution.py:279
  83.5 3.5 %collective-permute-start.16 = (bf16[256,256]{1,0:T(8,128)(2,1)S(1)}, bf16[256,256]{1,0:T(8,128)(2,1)S(1)}, u32[]{:S(2)}, u32[]{:S(2)}) collective-permute-start(bf16[256,256]{1,0:T(8,128)(2,1)S(1)} %get-tuple-element.74), channel_id=1, source_target_pairs={{2,0},{4,2},{6,4},{8,6},{10,8},{12,10},{14,12},{0,14},{3,1},{5,3},... | collective-permute-start | bytes 393224 | tf_op jit(solution)/shard_map/ppermute | solution.py:285
  87.1 3.5 %collective-permute-start.10 = (bf16[256,256]{1,0:T(8,128)(2,1)S(1)}, bf16[256,256]{1,0:T(8,128)(2,1)S(1)}, u32[]{:S(2)}, u32[]{:S(2)}) collective-permute-start(bf16[256,256]{1,0:T(8,128)(2,1)S(1)} %add_convert_fusion.19), channel_id=1, source_target_pairs={{0,1},{1,0},{2,3},{3,2},{4,5},{5,4},{6,7},{7,6},{8,9},{9,8},{10,11... | collective-permute-start | bytes 393224 | tf_op jit(solution)/shard_map/ppermute | solution.py:279
  90.6 2.9 %collective-permute-done.19 = bf16[256,256]{1,0:T(8,128)(2,1)S(1)} collective-permute-done((bf16[256,256]{1,0:T(8,128)(2,1)S(1)}, bf16[256,256]{1,0:T(8,128)(2,1)S(1)}, u32[]{:S(2)}, u32[]{:S(2)}) %collective-permute-start.19) | collective-permute-done | bytes 131104 | tf_op jit(solution)/shard_map/ppermute | solution.py:282
  95.3 7.9 %collective-permute-start.21 = (bf16[256,256]{1,0:T(8,128)(2,1)S(1)}, bf16[256,256]{1,0:T(8,128)(2,1)S(1)}, u32[]{:S(2)}, u32[]{:S(2)}) collective-permute-start(bf16[256,256]{1,0:T(8,128)(2,1)S(1)} %add_convert_fusion.5), channel_id=1, source_target_pairs={{0,16},{16,0},{1,17},{17,1},{2,18},{18,2},{3,19},{19,3},{4,20},{20... | collective-permute-start | bytes 393224 | tf_op jit(solution)/shard_map/ppermute | solution.py:279
  104.2 3.1 %node.1 = (bf16[256,512]{1,0:T(8,128)(2,1)}, bf16[512,128]{1,0:T(8,128)(2,1)S(1)}, bf16[512,128]{1,0:T(8,128)(2,1)S(1)}, f32[256,512]{1,0:T(8,128)S(1)}, f32[16,1536]{1,0:T(8,128)S(1)}) custom-call(s32[3]{0:T(128)S(1)} %pad_add_fusion.3.refs_0_.here, bf16[256,512]{1,0:T(8,128)(2,1)S(1)} %copy-done.4, bf16[256,512]{1,0:T(8,128)(2,1)S(1)} %copy-done.8, ...), custom_call_target="tpu_custom_call" | custom-call | bytes 3817484 | tf_op jit(solution)/shard_map/node/pallas_call | solution.py:47
  111.3 3.8 %collective-permute-done.23 = bf16[512,128]{1,0:T(8,128)(2,1)S(1)} collective-permute-done((bf16[512,128]{1,0:T(8,128)(2,1)S(1)}, bf16[512,128]{1,0:T(8,128)(2,1)S(1)}, u32[]{:S(2)}, u32[]{:S(2)}) %collective-permute-start.23) | collective-permute-done | bytes 131104 | tf_op jit(solution)/shard_map/ppermute | solution.py:279
  119.2 4.7 %collective-permute-done.28.refs_10_ = bf16[1024,128]{1,0:T(8,128)(2,1)S(1)} collective-permute-done((bf16[1024,128]{1,0:T(8,128)(2,1)S(1)}, bf16[1024,128]{1,0:T(8,128)(2,1)S(1)}, u32[]{:S(2)}, u32[]{:S(2)}) %collective-permute-start.28) | collective-permute-done | bytes 262176 | tf_op jit(solution)/shard_map/ppermute | solution.py:285
  126.8 3.3 %collective-permute-done.29.refs_12_ = bf16[1024,128]{1,0:T(8,128)(2,1)S(1)} collective-permute-done((bf16[1024,128]{1,0:T(8,128)(2,1)S(1)}, bf16[1024,128]{1,0:T(8,128)(2,1)S(1)}, u32[]{:S(2)}, u32[]{:S(2)}) %collective-permute-start.29) | collective-permute-done | bytes 262176 | tf_op jit(solution)/shard_map/ppermute | solution.py:285
  130.1 3.4 %collective-permute-start.30 = (bf16[1024,128]{1,0:T(8,128)(2,1)S(1)}, bf16[1024,128]{1,0:T(8,128)(2,1)S(1)}, u32[]{:S(2)}, u32[]{:S(2)}) collective-permute-start(bf16[1024,128]{1,0:T(8,128)(2,1)S(1)} %collective-permute-done.29.refs_12_), channel_id=1, source_target_pairs={{2,0},{4,2},{6,4},{8,6},{10,8},{12,10},{14,12},{0,14},{3,1},{5,3},... | collective-permute-start | bytes 786440 | tf_op jit(solution)/shard_map/ppermute | solution.py:285
  133.5 3.5 %collective-permute-start.31 = (bf16[32,128,128]{2,1,0:T(8,128)(2,1)S(1)}, bf16[32,128,128]{2,1,0:T(8,128)(2,1)S(1)}, u32[]{:S(2)}, u32[]{:S(2)}) collective-permute-start(bf16[32,128,128]{2,1,0:T(8,128)(2,1)S(1)} %collective-permute-done.20.refs_4_), channel_id=1, source_target_pairs={{0,16},{16,0},{1,17},{17,1},{2,18},{18,2},{3,19},{19,3},{4,20},{20... | collective-permute-start | bytes 3145736 | tf_op jit(solution)/shard_map/ppermute | solution.py:279
  137.0 3.2 %collective-permute-done.27.refs_13_ = bf16[1024,128]{1,0:T(8,128)(2,1)S(1)} collective-permute-done((bf16[1024,128]{1,0:T(8,128)(2,1)S(1)}, bf16[1024,128]{1,0:T(8,128)(2,1)S(1)}, u32[]{:S(2)}, u32[]{:S(2)}) %collective-permute-start.27) | collective-permute-done | bytes 262176 | tf_op jit(solution)/shard_map/ppermute | solution.py:282
  140.2 4.4 %collective-permute-start.32 = (bf16[32,128,128]{2,1,0:T(8,128)(2,1)S(1)}, bf16[32,128,128]{2,1,0:T(8,128)(2,1)S(1)}, u32[]{:S(2)}, u32[]{:S(2)}) collective-permute-start(bf16[32,128,128]{2,1,0:T(8,128)(2,1)S(1)} %collective-permute-done.24.refs_5_), channel_id=1, source_target_pairs={{0,16},{16,0},{1,17},{17,1},{2,18},{18,2},{3,19},{19,3},{4,20},{20... | collective-permute-start | bytes 3145736 | tf_op jit(solution)/shard_map/ppermute | solution.py:279
  144.6 9.1 %collective-permute-done.33.refs_15_ = bf16[1024,128]{1,0:T(8,128)(2,1)S(1)} collective-permute-done((bf16[1024,128]{1,0:T(8,128)(2,1)S(1)}, bf16[1024,128]{1,0:T(8,128)(2,1)S(1)}, u32[]{:S(2)}, u32[]{:S(2)}) %collective-permute-start.33) | collective-permute-done | bytes 262176 | tf_op jit(solution)/shard_map/ppermute | solution.py:282
  153.8 6.8 %tiles_back.1 = bf16[8192,128]{1,0:T(8,128)(2,1)S(1)} custom-call(s32[3]{0:T(128)S(1)} %pad_add_fusion.3.refs_0_.here, s32[4,256]{1,0:T(4,128)S(1)} %pad_add_fusion.refs_1_, bf16[64,128,128]{2,1,0:T(8,128)(2,1)S(1)} %bitcast.26, bf16[64,128,128]{2,1,0:T(8,128)(2,1)} %collective-permute-done.2.refs_3_, ...), custom_call_target="tpu_custom_call" | custom-call | flops 1073741824 | bytes 12587020 | tf_op jit(solution)/shard_map/tiles_back/pallas_call | solution.py:47
  161.9 7.3 %all-to-all-start.1 = ((bf16[32,256,128]{2,1,0:T(8,128)(2,1)}), bf16[32,256,128]{2,1,0:T(8,128)(2,1)S(1)}, u32[]{:S(2)}, u32[]{:S(2)}) async-start(bf16[32,256,128]{2,1,0:T(8,128)(2,1)} %bitcast.27), calls=%async_computation.1 | async-start | bytes 4194304 | tf_op jit(solution)/shard_map/all_to_all | solution.py:237
  169.8 27.6 %all-to-all-done.1.parts = bf16[32,256,128]{2,1,0:T(8,128)(2,1)S(1)} async-done(((bf16[32,256,128]{2,1,0:T(8,128)(2,1)}), bf16[32,256,128]{2,1,0:T(8,128)(2,1)S(1)}, u32[]{:S(2)}, u32[]{:S(2)}) %all-to-all-start.1) | async-done | bytes 2097184 | tf_op jit(solution)/shard_map/all_to_all | solution.py:237
  199.9 12.5 %all_to_all.38 = bf16[32,16,128]{2,1,0:T(8,128)(2,1)S(1)} all-to-all(bf16[32,16,128]{2,1,0:T(8,128)(2,1)S(1)} %bitcast.38), channel_id=1, replica_groups=mesh['xly'=8,'co'=2,'z'=8,'xh'=2] {'xly','co','xh'}, dimensions={0} | all-to-all | bytes 262144 | tf_op jit(solution)/shard_map/all_to_all | solution.py:237
  212.5 11.4 %all_to_all.39 = bf16[8,16,128]{2,1,0:T(8,128)(2,1)S(1)} all-to-all(bf16[8,16,128]{2,1,0:T(8,128)(2,1)S(1)} %broadcast_in_dim.4), channel_id=1, replica_groups=mesh['xly'=8,'co'=2,'z'=8,'xh'=2] {'z'}, dimensions={0} | all-to-all | bytes 65536 | tf_op jit(solution)/shard_map/all_to_all | solution.py:237
  223.9 12.6 %all_to_all.40 = bf16[32,16,128]{2,1,0:T(8,128)(2,1)S(1)} all-to-all(bf16[32,16,128]{2,1,0:T(8,128)(2,1)S(1)} %broadcast_in_dim.5), channel_id=1, replica_groups=mesh['xly'=8,'co'=2,'z'=8,'xh'=2] {'xly','co','xh'}, dimensions={0} | all-to-all | bytes 262144 | tf_op jit(solution)/shard_map/all_to_all | solution.py:237
  (124 shorter events, 60.3 us)
Async XLA Ops:
  0.6 41.3 %collective-permute-start.2 = (bf16[64,128,128]{2,1,0:T(8,128)(2,1)}, bf16[64,128,128]{2,1,0:T(8,128)(2,1)}, u32[]{:S(2)}, u32[]{:S(2)}) collective-permute-start(bf16[64,128,128]{2,1,0:T(8,128)(2,1)} %bitcast.24), channel_id=1, source_target_pairs={{0,16},{16,0},{1,17},{17,1},{2,18},{18,2},{3,19},{19,3},{4,20},{20... | collective-permute-start | bytes 6291464 | tf_op jit(solution)/shard_map/ppermute | solution.py:279
  9.4 32.6 %all-to-all-start = ((bf16[16,256,256]{2,1,0:T(8,128)(2,1)}), bf16[16,256,256]{2,1,0:T(8,128)(2,1)}, u32[]{:S(2)}, u32[]{:S(2)}) async-start(bf16[16,256,256]{2,1,0:T(8,128)(2,1)} %copy-done.1), calls=%async_computation | async-start | bytes 4194304 | tf_op jit(solution)/shard_map/all_to_all | solution.py:237
  16.0 24.9 %collective-permute-start.1 = (s32[2,256]{1,0:T(2,128)S(1)}, s32[2,256]{1,0:T(2,128)S(1)}, u32[]{:S(2)}, u32[]{:S(2)}) collective-permute-start(s32[2,256]{1,0:T(2,128)S(1)} %pad_add_fusion.1), channel_id=1, source_target_pairs={{0,1},{1,0},{2,3},{3,2},{4,5},{5,4},{6,7},{7,6},{8,9},{9,8},{10,11... | collective-permute-start | bytes 6152 | tf_op jit(solution)/shard_map/ppermute | solution.py:279
  47.5 10.5 %collective-permute-start.3 = (bf16[512,256]{1,0:T(8,128)(2,1)S(1)}, bf16[512,256]{1,0:T(8,128)(2,1)S(1)}, u32[]{:S(2)}, u32[]{:S(2)}) collective-permute-start(bf16[512,256]{1,0:T(8,128)(2,1)S(1)} %get-tuple-element.40), channel_id=1, source_target_pairs={{0,2},{2,4},{4,6},{6,8},{8,10},{10,12},{12,14},{14,0},{1,3},{3,5},... | collective-permute-start | bytes 786440 | tf_op jit(solution)/shard_map/ppermute | solution.py:282
  49.5 8.6 %collective-permute-start.7 = (bf16[512,256]{1,0:T(8,128)(2,1)S(1)}, bf16[512,256]{1,0:T(8,128)(2,1)S(1)}, u32[]{:S(2)}, u32[]{:S(2)}) collective-permute-start(bf16[512,256]{1,0:T(8,128)(2,1)S(1)} %get-tuple-element.44), channel_id=1, source_target_pairs={{2,0},{4,2},{6,4},{8,6},{10,8},{12,10},{14,12},{0,14},{3,1},{5,3},... | collective-permute-start | bytes 786440 | tf_op jit(solution)/shard_map/ppermute | solution.py:285
  52.3 13.8 %collective-permute-start.12 = (bf16[1024,256]{1,0:T(8,128)(2,1)S(1)}, bf16[1024,256]{1,0:T(8,128)(2,1)S(1)}, u32[]{:S(2)}, u32[]{:S(2)}) collective-permute-start(bf16[1024,256]{1,0:T(8,128)(2,1)S(1)} %get-tuple-element.50), channel_id=1, source_target_pairs={{0,1},{1,0},{2,3},{3,2},{4,5},{5,4},{6,7},{7,6},{8,9},{9,8},{10,11... | collective-permute-start | bytes 1572872 | tf_op jit(solution)/shard_map/ppermute | solution.py:279
  54.8 22.5 %collective-permute-start.11 = (bf16[1024,256]{1,0:T(8,128)(2,1)S(1)}, bf16[1024,256]{1,0:T(8,128)(2,1)S(1)}, u32[]{:S(2)}, u32[]{:S(2)}) collective-permute-start(bf16[1024,256]{1,0:T(8,128)(2,1)S(1)} %get-tuple-element.48), channel_id=1, source_target_pairs={{0,1},{1,0},{2,3},{3,2},{4,5},{5,4},{6,7},{7,6},{8,9},{9,8},{10,11... | collective-permute-start | bytes 1572872 | tf_op jit(solution)/shard_map/ppermute | solution.py:279
  58.1 9.7 %collective-permute-start.4 = (bf16[512,256]{1,0:T(8,128)(2,1)S(1)}, bf16[512,256]{1,0:T(8,128)(2,1)S(1)}, u32[]{:S(2)}, u32[]{:S(2)}) collective-permute-start(bf16[512,256]{1,0:T(8,128)(2,1)S(1)} %add_convert_fusion.4), channel_id=1, source_target_pairs={{0,2},{2,4},{4,6},{6,8},{8,10},{10,12},{12,14},{14,0},{1,3},{3,5},... | collective-permute-start | bytes 786440 | tf_op jit(solution)/shard_map/ppermute | solution.py:282
  58.3 15.2 %collective-permute-start.8 = (bf16[512,256]{1,0:T(8,128)(2,1)S(1)}, bf16[512,256]{1,0:T(8,128)(2,1)S(1)}, u32[]{:S(2)}, u32[]{:S(2)}) collective-permute-start(bf16[512,256]{1,0:T(8,128)(2,1)S(1)} %add_convert_fusion.1), channel_id=1, source_target_pairs={{2,0},{4,2},{6,4},{8,6},{10,8},{12,10},{14,12},{0,14},{3,1},{5,3},... | collective-permute-start | bytes 786440 | tf_op jit(solution)/shard_map/ppermute | solution.py:285
  67.8 12.3 %collective-permute-start.5 = (bf16[512,256]{1,0:T(8,128)(2,1)S(1)}, bf16[512,256]{1,0:T(8,128)(2,1)S(1)}, u32[]{:S(2)}, u32[]{:S(2)}) collective-permute-start(bf16[512,256]{1,0:T(8,128)(2,1)S(1)} %add_convert_fusion.3), channel_id=1, source_target_pairs={{0,2},{2,4},{4,6},{6,8},{8,10},{10,12},{12,14},{14,0},{1,3},{3,5},... | collective-permute-start | bytes 786440 | tf_op jit(solution)/shard_map/ppermute | solution.py:282
  73.6 13.4 %collective-permute-start.9 = (bf16[512,256]{1,0:T(8,128)(2,1)S(1)}, bf16[512,256]{1,0:T(8,128)(2,1)S(1)}, u32[]{:S(2)}, u32[]{:S(2)}) collective-permute-start(bf16[512,256]{1,0:T(8,128)(2,1)S(1)} %add_convert_fusion), channel_id=1, source_target_pairs={{2,0},{4,2},{6,4},{8,6},{10,8},{12,10},{14,12},{0,14},{3,1},{5,3},... | collective-permute-start | bytes 786440 | tf_op jit(solution)/shard_map/ppermute | solution.py:285
  74.5 20.8 %collective-permute-start.20 = (bf16[32,128,128]{2,1,0:T(8,128)(2,1)S(1)}, bf16[32,128,128]{2,1,0:T(8,128)(2,1)S(1)}, u32[]{:S(2)}, u32[]{:S(2)}) collective-permute-start(bf16[32,128,128]{2,1,0:T(8,128)(2,1)S(1)} %get-tuple-element.58), channel_id=1, source_target_pairs={{0,1},{1,0},{2,3},{3,2},{4,5},{5,4},{6,7},{7,6},{8,9},{9,8},{10,11... | collective-permute-start | bytes 3145736 | tf_op jit(solution)/shard_map/ppermute | solution.py:279
  80.2 6.8 %collective-permute-start.6 = (bf16[512,256]{1,0:T(8,128)(2,1)S(1)}, bf16[512,256]{1,0:T(8,128)(2,1)S(1)}, u32[]{:S(2)}, u32[]{:S(2)}) collective-permute-start(bf16[512,256]{1,0:T(8,128)(2,1)S(1)} %add_convert_fusion.2), channel_id=1, source_target_pairs={{0,2},{2,4},{4,6},{6,8},{8,10},{10,12},{12,14},{14,0},{1,3},{3,5},... | collective-permute-start | bytes 786440 | tf_op jit(solution)/shard_map/ppermute | solution.py:282
  83.5 7.1 %collective-permute-start.16 = (bf16[256,256]{1,0:T(8,128)(2,1)S(1)}, bf16[256,256]{1,0:T(8,128)(2,1)S(1)}, u32[]{:S(2)}, u32[]{:S(2)}) collective-permute-start(bf16[256,256]{1,0:T(8,128)(2,1)S(1)} %get-tuple-element.74), channel_id=1, source_target_pairs={{2,0},{4,2},{6,4},{8,6},{10,8},{12,10},{14,12},{0,14},{3,1},{5,3},... | collective-permute-start | bytes 393224 | tf_op jit(solution)/shard_map/ppermute | solution.py:285
  87.1 16.1 %collective-permute-start.10 = (bf16[256,256]{1,0:T(8,128)(2,1)S(1)}, bf16[256,256]{1,0:T(8,128)(2,1)S(1)}, u32[]{:S(2)}, u32[]{:S(2)}) collective-permute-start(bf16[256,256]{1,0:T(8,128)(2,1)S(1)} %add_convert_fusion.19), channel_id=1, source_target_pairs={{0,1},{1,0},{2,3},{3,2},{4,5},{5,4},{6,7},{7,6},{8,9},{9,8},{10,11... | collective-permute-start | bytes 393224 | tf_op jit(solution)/shard_map/ppermute | solution.py:279
  95.3 8.9 %collective-permute-start.21 = (bf16[256,256]{1,0:T(8,128)(2,1)S(1)}, bf16[256,256]{1,0:T(8,128)(2,1)S(1)}, u32[]{:S(2)}, u32[]{:S(2)}) collective-permute-start(bf16[256,256]{1,0:T(8,128)(2,1)S(1)} %add_convert_fusion.5), channel_id=1, source_target_pairs={{0,16},{16,0},{1,17},{17,1},{2,18},{18,2},{3,19},{19,3},{4,20},{20... | collective-permute-start | bytes 393224 | tf_op jit(solution)/shard_map/ppermute | solution.py:279
  115.1 25.2 %collective-permute-start.24 = (bf16[32,128,128]{2,1,0:T(8,128)(2,1)S(1)}, bf16[32,128,128]{2,1,0:T(8,128)(2,1)S(1)}, u32[]{:S(2)}, u32[]{:S(2)}) collective-permute-start(bf16[32,128,128]{2,1,0:T(8,128)(2,1)S(1)} %get-tuple-element.64), channel_id=1, source_target_pairs={{0,1},{1,0},{2,3},{3,2},{4,5},{5,4},{6,7},{7,6},{8,9},{9,8},{10,11... | collective-permute-start | bytes 3145736 | tf_op jit(solution)/shard_map/ppermute | solution.py:279
  119.2 7.5 %collective-permute-start.25 = (bf16[1024,128]{1,0:T(8,128)(2,1)S(1)}, bf16[1024,128]{1,0:T(8,128)(2,1)S(1)}, u32[]{:S(2)}, u32[]{:S(2)}) collective-permute-start(bf16[1024,128]{1,0:T(8,128)(2,1)S(1)} %bitcast.29), channel_id=1, source_target_pairs={{0,2},{2,4},{4,6},{6,8},{8,10},{10,12},{12,14},{14,0},{1,3},{3,5},... | collective-permute-start | bytes 786440 | tf_op jit(solution)/shard_map/ppermute | solution.py:282
  126.8 6.7 %collective-permute-start.26 = (bf16[1024,128]{1,0:T(8,128)(2,1)S(1)}, bf16[1024,128]{1,0:T(8,128)(2,1)S(1)}, u32[]{:S(2)}, u32[]{:S(2)}) collective-permute-start(bf16[1024,128]{1,0:T(8,128)(2,1)S(1)} %collective-permute-done.25.refs_9_), channel_id=1, source_target_pairs={{0,2},{2,4},{4,6},{6,8},{8,10},{10,12},{12,14},{14,0},{1,3},{3,5},... | collective-permute-start | bytes 786440 | tf_op jit(solution)/shard_map/ppermute | solution.py:282
  130.1 6.9 %collective-permute-start.30 = (bf16[1024,128]{1,0:T(8,128)(2,1)S(1)}, bf16[1024,128]{1,0:T(8,128)(2,1)S(1)}, u32[]{:S(2)}, u32[]{:S(2)}) collective-permute-start(bf16[1024,128]{1,0:T(8,128)(2,1)S(1)} %collective-permute-done.29.refs_12_), channel_id=1, source_target_pairs={{2,0},{4,2},{6,4},{8,6},{10,8},{12,10},{14,12},{0,14},{3,1},{5,3},... | collective-permute-start | bytes 786440 | tf_op jit(solution)/shard_map/ppermute | solution.py:285
  133.5 11.1 %collective-permute-start.31 = (bf16[32,128,128]{2,1,0:T(8,128)(2,1)S(1)}, bf16[32,128,128]{2,1,0:T(8,128)(2,1)S(1)}, u32[]{:S(2)}, u32[]{:S(2)}) collective-permute-start(bf16[32,128,128]{2,1,0:T(8,128)(2,1)S(1)} %collective-permute-done.20.refs_4_), channel_id=1, source_target_pairs={{0,16},{16,0},{1,17},{17,1},{2,18},{18,2},{3,19},{19,3},{4,20},{20... | collective-permute-start | bytes 3145736 | tf_op jit(solution)/shard_map/ppermute | solution.py:279
  140.2 13.5 %collective-permute-start.32 = (bf16[32,128,128]{2,1,0:T(8,128)(2,1)S(1)}, bf16[32,128,128]{2,1,0:T(8,128)(2,1)S(1)}, u32[]{:S(2)}, u32[]{:S(2)}) collective-permute-start(bf16[32,128,128]{2,1,0:T(8,128)(2,1)S(1)} %collective-permute-done.24.refs_5_), channel_id=1, source_target_pairs={{0,16},{16,0},{1,17},{17,1},{2,18},{18,2},{3,19},{19,3},{4,20},{20... | collective-permute-start | bytes 3145736 | tf_op jit(solution)/shard_map/ppermute | solution.py:279
  144.6 9.1 %collective-permute-start.33 = (bf16[1024,128]{1,0:T(8,128)(2,1)S(1)}, bf16[1024,128]{1,0:T(8,128)(2,1)S(1)}, u32[]{:S(2)}, u32[]{:S(2)}) collective-permute-start(bf16[1024,128]{1,0:T(8,128)(2,1)S(1)} %collective-permute-done.27.refs_13_), channel_id=1, source_target_pairs={{0,2},{2,4},{4,6},{6,8},{8,10},{10,12},{12,14},{14,0},{1,3},{3,5},... | collective-permute-start | bytes 786440 | tf_op jit(solution)/shard_map/ppermute | solution.py:282
  161.9 35.5 %all-to-all-start.1 = ((bf16[32,256,128]{2,1,0:T(8,128)(2,1)}), bf16[32,256,128]{2,1,0:T(8,128)(2,1)S(1)}, u32[]{:S(2)}, u32[]{:S(2)}) async-start(bf16[32,256,128]{2,1,0:T(8,128)(2,1)} %bitcast.27), calls=%async_computation.1 | async-start | bytes 4194304 | tf_op jit(solution)/shard_map/all_to_all | solution.py:237
  (29 other events, 365.7 us)

commit v4 on v3

--- a/solution.py
+++ b/solution.py
@@ -387,7 +387,7 @@
         if k <= n_down:
             shards[k] = down(shards[k - 1])
 
-    late = [1 - n_up, n_down] if n_down else [0]
+    late = [-n_up, n_down] if n_down else [0]
     tiles_x[1] = lax.optimization_barrier([tiles_x[1]] + [shards[d] for d in late])[0]
     tiles_cx.append(swap(tiles_x[1], "co"))
 

time: 239 us -> 237 us (level)
  waiting for transfers between devices: 99.5 us -> 94.7 us
  starting transfers between devices: 72.2 us -> 76 us
    ppermute x10, waiting for transfers between devices: 11.7 us -> 5.69 us  [down(): return lax.ppermute(values, 'z', [((i + 1) % n_z, i) for i in range(n_z)])]
    ppermute x13, waiting for transfers between devices: 36.6 us -> 40.5 us  [swap(): return lax.ppermute(values, axis, [(0, 1), (1, 0)])]
    ppermute x11, waiting for transfers between devices: 22.6 us -> 19.7 us  [up(): return lax.ppermute(values, 'z', [(i, (i + 1) % n_z) for i in range(n_z)])]
  transfers between devices with their start and end apart: 36 -> 36, of which waited for: 21 -> 24; matrix products, arithmetic and copies ran while one was open for 1% -> 1% of each run, Pallas kernels for 0% -> 0%
where the time goes in v4:
time: 237 us
  waiting for transfers between devices  94.7 us (40%)
  starting transfers between devices  76 us (32%)
  blocking collectives  38 us (16%)
  Pallas kernels  17.1 us (7%)
  local copies, waits for them, and re-layouts  8.05 us (3%)
    ppermute x13, waiting for transfers between devices, swap(): return lax.ppermute(values, axis, [(0, 1), (1, 0)])  40.5 us
    all_to_all x3, blocking collectives, exchange(): return lax.all_to_all(flat, axes, split_axis=0, concat_axis=0, tiled=True)  38 us
    ppermute x13, starting transfers between devices, swap(): return lax.ppermute(values, axis, [(0, 1), (1, 0)])  36.5 us
    all_to_all x2, waiting for transfers between devices, exchange(): return lax.all_to_all(flat, axes, split_axis=0, concat_axis=0, tiled=True)  28.7 us
    ppermute x10, starting transfers between devices, down(): return lax.ppermute(values, 'z', [((i + 1) % n_z, i) for i in range(n_z)])  23.6 us
    ppermute x11, waiting for transfers between devices, up(): return lax.ppermute(values, 'z', [(i, (i + 1) % n_z) for i in range(n_z)])  19.7 us
    pallas_call x5, Pallas kernels, call(): pl.pallas_call(kernel, out_shape=out_shape, in_specs=[pl.BlockSpec(memory...  17.1 us
    all_to_all x2, starting transfers between devices, exchange(): return lax.all_to_all(flat, axes, split_axis=0, concat_axis=0, tiled=True)  13.2 us
  transfers between devices with their start and end apart: 36, of which 24 were waited for; matrix products, arithmetic and copies ran while one was open for 1% of the time, Pallas kernels for 0%

profile of v4, /device:TPU:1, one launch (start us, length us, event | category | flops | bytes accessed | tf_op | source)
XLA Modules:
  0.0 237.0 jit_solution(6137947973174135527)
XLA Ops:
  0.6 3.3 %collective-permute-start.2 = (bf16[64,128,128]{2,1,0:T(8,128)(2,1)}, bf16[64,128,128]{2,1,0:T(8,128)(2,1)}, u32[]{:S(2)}, u32[]{:S(2)}) collective-permute-start(bf16[64,128,128]{2,1,0:T(8,128)(2,1)} %bitcast.24), channel_id=1, source_target_pairs={{0,16},{16,0},{1,17},{17,1},{2,18},{18,2},{3,19},{19,3},{4,20},{20... | collective-permute-start | bytes 6291464 | tf_op jit(solution)/shard_map/ppermute | solution.py:279
  9.4 4.5 %all-to-all-start = ((bf16[16,256,256]{2,1,0:T(8,128)(2,1)}), bf16[16,256,256]{2,1,0:T(8,128)(2,1)}, u32[]{:S(2)}, u32[]{:S(2)}) async-start(bf16[16,256,256]{2,1,0:T(8,128)(2,1)} %copy-done.1), calls=%async_computation | async-start | bytes 4194304 | tf_op jit(solution)/shard_map/all_to_all | solution.py:237
  18.0 22.9 %collective-permute-done.1 = s32[2,256]{1,0:T(2,128)S(1)} collective-permute-done((s32[2,256]{1,0:T(2,128)S(1)}, s32[2,256]{1,0:T(2,128)S(1)}, u32[]{:S(2)}, u32[]{:S(2)}) %collective-permute-start.1) | collective-permute-done | bytes 2080 | tf_op jit(solution)/shard_map/ppermute | solution.py:279
  41.9 5.1 %tiles.1 = (bf16[1024,256]{1,0:T(8,128)(2,1)S(1)}, bf16[1024,256]{1,0:T(8,128)(2,1)S(1)}, bf16[512,256]{1,0:T(8,128)(2,1)S(1)}, bf16[512,256]{1,0:T(8,128)(2,1)S...) custom-call(s32[3]{0:T(128)S(1)} %pad_add_fusion.3.refs_0_.here, ...), custom_call_target="tpu_custom_call" | custom-call | flops 1073741824 | bytes 10489868 | tf_op jit(solution)/shard_map/tiles/pallas_call | solution.py:47
  49.1 3.6 %collective-permute-start.7 = (bf16[512,256]{1,0:T(8,128)(2,1)S(1)}, bf16[512,256]{1,0:T(8,128)(2,1)S(1)}, u32[]{:S(2)}, u32[]{:S(2)}) collective-permute-start(bf16[512,256]{1,0:T(8,128)(2,1)S(1)} %get-tuple-element.44), channel_id=1, source_target_pairs={{2,0},{4,2},{6,4},{8,6},{10,8},{12,10},{14,12},{0,14},{3,1},{5,3},... | collective-permute-start | bytes 786440 | tf_op jit(solution)/shard_map/ppermute | solution.py:285
  61.4 5.1 %collective-permute-done.12 = bf16[1024,256]{1,0:T(8,128)(2,1)S(1)} collective-permute-done((bf16[1024,256]{1,0:T(8,128)(2,1)S(1)}, bf16[1024,256]{1,0:T(8,128)(2,1)S(1)}, u32[]{:S(2)}, u32[]{:S(2)}) %collective-permute-start.12) | collective-permute-done | bytes 524320 | tf_op jit(solution)/shard_map/ppermute | solution.py:279
  73.8 2.8 %collective-permute-start.20 = (bf16[32,128,128]{2,1,0:T(8,128)(2,1)S(1)}, bf16[32,128,128]{2,1,0:T(8,128)(2,1)S(1)}, u32[]{:S(2)}, u32[]{:S(2)}) collective-permute-start(bf16[32,128,128]{2,1,0:T(8,128)(2,1)S(1)} %get-tuple-element.58), channel_id=1, source_target_pairs={{0,1},{1,0},{2,3},{3,2},{4,5},{5,4},{6,7},{7,6},{8,9},{9,8},{10,11... | collective-permute-start | bytes 3145736 | tf_op jit(solution)/shard_map/ppermute | solution.py:279
  77.8 2.7 %collective-permute-start.15 = (bf16[256,256]{1,0:T(8,128)(2,1)S(1)}, bf16[256,256]{1,0:T(8,128)(2,1)S(1)}, u32[]{:S(2)}, u32[]{:S(2)}) collective-permute-start(bf16[256,256]{1,0:T(8,128)(2,1)S(1)} %add_convert_fusion.13), channel_id=1, source_target_pairs={{2,0},{4,2},{6,4},{8,6},{10,8},{12,10},{14,12},{0,14},{3,1},{5,3},... | collective-permute-start | bytes 393224 | tf_op jit(solution)/shard_map/ppermute | solution.py:285
  83.9 3.5 %collective-permute-start.16 = (bf16[256,256]{1,0:T(8,128)(2,1)S(1)}, bf16[256,256]{1,0:T(8,128)(2,1)S(1)}, u32[]{:S(2)}, u32[]{:S(2)}) collective-permute-start(bf16[256,256]{1,0:T(8,128)(2,1)S(1)} %get-tuple-element.74), channel_id=1, source_target_pairs={{2,0},{4,2},{6,4},{8,6},{10,8},{12,10},{14,12},{0,14},{3,1},{5,3},... | collective-permute-start | bytes 393224 | tf_op jit(solution)/shard_map/ppermute | solution.py:285
  87.6 3.6 %collective-permute-start.10 = (bf16[256,256]{1,0:T(8,128)(2,1)S(1)}, bf16[256,256]{1,0:T(8,128)(2,1)S(1)}, u32[]{:S(2)}, u32[]{:S(2)}) collective-permute-start(bf16[256,256]{1,0:T(8,128)(2,1)S(1)} %add_convert_fusion.19), channel_id=1, source_target_pairs={{0,1},{1,0},{2,3},{3,2},{4,5},{5,4},{6,7},{7,6},{8,9},{9,8},{10,11... | collective-permute-start | bytes 393224 | tf_op jit(solution)/shard_map/ppermute | solution.py:279
  91.2 2.9 %collective-permute-done.19 = bf16[256,256]{1,0:T(8,128)(2,1)S(1)} collective-permute-done((bf16[256,256]{1,0:T(8,128)(2,1)S(1)}, bf16[256,256]{1,0:T(8,128)(2,1)S(1)}, u32[]{:S(2)}, u32[]{:S(2)}) %collective-permute-start.19) | collective-permute-done | bytes 131104 | tf_op jit(solution)/shard_map/ppermute | solution.py:282
  96.5 7.1 %collective-permute-start.21 = (bf16[256,256]{1,0:T(8,128)(2,1)S(1)}, bf16[256,256]{1,0:T(8,128)(2,1)S(1)}, u32[]{:S(2)}, u32[]{:S(2)}) collective-permute-start(bf16[256,256]{1,0:T(8,128)(2,1)S(1)} %add_convert_fusion.5), channel_id=1, source_target_pairs={{0,16},{16,0},{1,17},{17,1},{2,18},{18,2},{3,19},{19,3},{4,20},{20... | collective-permute-start | bytes 393224 | tf_op jit(solution)/shard_map/ppermute | solution.py:279
  104.7 3.1 %node.1 = (bf16[256,512]{1,0:T(8,128)(2,1)}, bf16[512,128]{1,0:T(8,128)(2,1)S(1)}, bf16[512,128]{1,0:T(8,128)(2,1)S(1)}, f32[256,512]{1,0:T(8,128)S(1)}, f32[16,1536]{1,0:T(8,128)S(1)}) custom-call(s32[3]{0:T(128)S(1)} %pad_add_fusion.3.refs_0_.here, bf16[256,512]{1,0:T(8,128)(2,1)S(1)} %copy-done.4, bf16[256,512]{1,0:T(8,128)(2,1)S(1)} %copy-done.8, ...), custom_call_target="tpu_custom_call" | custom-call | bytes 3817484 | tf_op jit(solution)/shard_map/node/pallas_call | solution.py:47
  111.7 3.8 %collective-permute-done.23 = bf16[512,128]{1,0:T(8,128)(2,1)S(1)} collective-permute-done((bf16[512,128]{1,0:T(8,128)(2,1)S(1)}, bf16[512,128]{1,0:T(8,128)(2,1)S(1)}, u32[]{:S(2)}, u32[]{:S(2)}) %collective-permute-start.23) | collective-permute-done | bytes 131104 | tf_op jit(solution)/shard_map/ppermute | solution.py:279
  124.6 3.4 %collective-permute-start.30 = (bf16[1024,128]{1,0:T(8,128)(2,1)S(1)}, bf16[1024,128]{1,0:T(8,128)(2,1)S(1)}, u32[]{:S(2)}, u32[]{:S(2)}) collective-permute-start(bf16[1024,128]{1,0:T(8,128)(2,1)S(1)} %collective-permute-done.29.refs_10_), channel_id=1, source_target_pairs={{2,0},{4,2},{6,4},{8,6},{10,8},{12,10},{14,12},{0,14},{3,1},{5,3},... | collective-permute-start | bytes 786440 | tf_op jit(solution)/shard_map/ppermute | solution.py:285
  131.3 3.4 %collective-permute-start.31 = (bf16[1024,128]{1,0:T(8,128)(2,1)S(1)}, bf16[1024,128]{1,0:T(8,128)(2,1)S(1)}, u32[]{:S(2)}, u32[]{:S(2)}) collective-permute-start(bf16[1024,128]{1,0:T(8,128)(2,1)S(1)} %collective-permute-done.30.refs_12_), channel_id=1, source_target_pairs={{2,0},{4,2},{6,4},{8,6},{10,8},{12,10},{14,12},{0,14},{3,1},{5,3},... | collective-permute-start | bytes 786440 | tf_op jit(solution)/shard_map/ppermute | solution.py:285
  137.1 3.9 %collective-permute-start.32 = (bf16[32,128,128]{2,1,0:T(8,128)(2,1)S(1)}, bf16[32,128,128]{2,1,0:T(8,128)(2,1)S(1)}, u32[]{:S(2)}, u32[]{:S(2)}) collective-permute-start(bf16[32,128,128]{2,1,0:T(8,128)(2,1)S(1)} %collective-permute-done.20.refs_4_), channel_id=1, source_target_pairs={{0,16},{16,0},{1,17},{17,1},{2,18},{18,2},{3,19},{19,3},{4,20},{20... | collective-permute-start | bytes 3145736 | tf_op jit(solution)/shard_map/ppermute | solution.py:279
  143.5 5.0 %collective-permute-start.33 = (bf16[32,128,128]{2,1,0:T(8,128)(2,1)S(1)}, bf16[32,128,128]{2,1,0:T(8,128)(2,1)S(1)}, u32[]{:S(2)}, u32[]{:S(2)}) collective-permute-start(bf16[32,128,128]{2,1,0:T(8,128)(2,1)S(1)} %collective-permute-done.24.refs_5_), channel_id=1, source_target_pairs={{0,16},{16,0},{1,17},{17,1},{2,18},{18,2},{3,19},{19,3},{4,20},{20... | collective-permute-start | bytes 3145736 | tf_op jit(solution)/shard_map/ppermute | solution.py:279
  150.8 6.0 %tiles_back.1 = bf16[8192,128]{1,0:T(8,128)(2,1)S(1)} custom-call(s32[3]{0:T(128)S(1)} %pad_add_fusion.3.refs_0_.here, s32[4,256]{1,0:T(4,128)S(1)} %pad_add_fusion.refs_1_, bf16[64,128,128]{2,1,0:T(8,128)(2,1)S(1)} %bitcast.26, bf16[64,128,128]{2,1,0:T(8,128)(2,1)} %collective-permute-done.2.refs_3_, ...), custom_call_target="tpu_custom_call" | custom-call | flops 1073741824 | bytes 12587020 | tf_op jit(solution)/shard_map/tiles_back/pallas_call | solution.py:47
  158.2 8.7 %all-to-all-start.1 = ((bf16[32,256,128]{2,1,0:T(8,128)(2,1)}), bf16[32,256,128]{2,1,0:T(8,128)(2,1)S(1)}, u32[]{:S(2)}, u32[]{:S(2)}) async-start(bf16[32,256,128]{2,1,0:T(8,128)(2,1)} %bitcast.27), calls=%async_computation.1 | async-start | bytes 4194304 | tf_op jit(solution)/shard_map/all_to_all | solution.py:237
  167.5 27.6 %all-to-all-done.1.parts = bf16[32,256,128]{2,1,0:T(8,128)(2,1)S(1)} async-done(((bf16[32,256,128]{2,1,0:T(8,128)(2,1)}), bf16[32,256,128]{2,1,0:T(8,128)(2,1)S(1)}, u32[]{:S(2)}, u32[]{:S(2)}) %all-to-all-start.1) | async-done | bytes 2097184 | tf_op jit(solution)/shard_map/all_to_all | solution.py:237
  197.6 12.5 %all_to_all.38 = bf16[32,16,128]{2,1,0:T(8,128)(2,1)S(1)} all-to-all(bf16[32,16,128]{2,1,0:T(8,128)(2,1)S(1)} %bitcast.38), channel_id=1, replica_groups=mesh['xly'=8,'co'=2,'z'=8,'xh'=2] {'xly','co','xh'}, dimensions={0} | all-to-all | bytes 262144 | tf_op jit(solution)/shard_map/all_to_all | solution.py:237
  210.2 12.9 %all_to_all.39 = bf16[8,16,128]{2,1,0:T(8,128)(2,1)S(1)} all-to-all(bf16[8,16,128]{2,1,0:T(8,128)(2,1)S(1)} %broadcast_in_dim.4), channel_id=1, replica_groups=mesh['xly'=8,'co'=2,'z'=8,'xh'=2] {'z'}, dimensions={0} | all-to-all | bytes 65536 | tf_op jit(solution)/shard_map/all_to_all | solution.py:237
  223.1 12.6 %all_to_all.40 = bf16[32,16,128]{2,1,0:T(8,128)(2,1)S(1)} all-to-all(bf16[32,16,128]{2,1,0:T(8,128)(2,1)S(1)} %broadcast_in_dim.5), channel_id=1, replica_groups=mesh['xly'=8,'co'=2,'z'=8,'xh'=2] {'xly','co','xh'}, dimensions={0} | all-to-all | bytes 262144 | tf_op jit(solution)/shard_map/all_to_all | solution.py:237
  (124 shorter events, 65.3 us)
Async XLA Ops:
  0.6 41.3 %collective-permute-start.2 = (bf16[64,128,128]{2,1,0:T(8,128)(2,1)}, bf16[64,128,128]{2,1,0:T(8,128)(2,1)}, u32[]{:S(2)}, u32[]{:S(2)}) collective-permute-start(bf16[64,128,128]{2,1,0:T(8,128)(2,1)} %bitcast.24), channel_id=1, source_target_pairs={{0,16},{16,0},{1,17},{17,1},{2,18},{18,2},{3,19},{19,3},{4,20},{20... | collective-permute-start | bytes 6291464 | tf_op jit(solution)/shard_map/ppermute | solution.py:279
  9.4 32.6 %all-to-all-start = ((bf16[16,256,256]{2,1,0:T(8,128)(2,1)}), bf16[16,256,256]{2,1,0:T(8,128)(2,1)}, u32[]{:S(2)}, u32[]{:S(2)}) async-start(bf16[16,256,256]{2,1,0:T(8,128)(2,1)} %copy-done.1), calls=%async_computation | async-start | bytes 4194304 | tf_op jit(solution)/shard_map/all_to_all | solution.py:237
  16.0 24.9 %collective-permute-start.1 = (s32[2,256]{1,0:T(2,128)S(1)}, s32[2,256]{1,0:T(2,128)S(1)}, u32[]{:S(2)}, u32[]{:S(2)}) collective-permute-start(s32[2,256]{1,0:T(2,128)S(1)} %pad_add_fusion.1), channel_id=1, source_target_pairs={{0,1},{1,0},{2,3},{3,2},{4,5},{5,4},{6,7},{7,6},{8,9},{9,8},{10,11... | collective-permute-start | bytes 6152 | tf_op jit(solution)/shard_map/ppermute | solution.py:279
  47.1 11.3 %collective-permute-start.3 = (bf16[512,256]{1,0:T(8,128)(2,1)S(1)}, bf16[512,256]{1,0:T(8,128)(2,1)S(1)}, u32[]{:S(2)}, u32[]{:S(2)}) collective-permute-start(bf16[512,256]{1,0:T(8,128)(2,1)S(1)} %get-tuple-element.40), channel_id=1, source_target_pairs={{0,2},{2,4},{4,6},{6,8},{8,10},{10,12},{12,14},{14,0},{1,3},{3,5},... | collective-permute-start | bytes 786440 | tf_op jit(solution)/shard_map/ppermute | solution.py:282
  49.1 9.4 %collective-permute-start.7 = (bf16[512,256]{1,0:T(8,128)(2,1)S(1)}, bf16[512,256]{1,0:T(8,128)(2,1)S(1)}, u32[]{:S(2)}, u32[]{:S(2)}) collective-permute-start(bf16[512,256]{1,0:T(8,128)(2,1)S(1)} %get-tuple-element.44), channel_id=1, source_target_pairs={{2,0},{4,2},{6,4},{8,6},{10,8},{12,10},{14,12},{0,14},{3,1},{5,3},... | collective-permute-start | bytes 786440 | tf_op jit(solution)/shard_map/ppermute | solution.py:285
  52.7 13.8 %collective-permute-start.12 = (bf16[1024,256]{1,0:T(8,128)(2,1)S(1)}, bf16[1024,256]{1,0:T(8,128)(2,1)S(1)}, u32[]{:S(2)}, u32[]{:S(2)}) collective-permute-start(bf16[1024,256]{1,0:T(8,128)(2,1)S(1)} %get-tuple-element.50), channel_id=1, source_target_pairs={{0,1},{1,0},{2,3},{3,2},{4,5},{5,4},{6,7},{7,6},{8,9},{9,8},{10,11... | collective-permute-start | bytes 1572872 | tf_op jit(solution)/shard_map/ppermute | solution.py:279
  55.3 22.4 %collective-permute-start.11 = (bf16[1024,256]{1,0:T(8,128)(2,1)S(1)}, bf16[1024,256]{1,0:T(8,128)(2,1)S(1)}, u32[]{:S(2)}, u32[]{:S(2)}) collective-permute-start(bf16[1024,256]{1,0:T(8,128)(2,1)S(1)} %get-tuple-element.48), channel_id=1, source_target_pairs={{0,1},{1,0},{2,3},{3,2},{4,5},{5,4},{6,7},{7,6},{8,9},{9,8},{10,11... | collective-permute-start | bytes 1572872 | tf_op jit(solution)/shard_map/ppermute | solution.py:279
  58.5 9.6 %collective-permute-start.4 = (bf16[512,256]{1,0:T(8,128)(2,1)S(1)}, bf16[512,256]{1,0:T(8,128)(2,1)S(1)}, u32[]{:S(2)}, u32[]{:S(2)}) collective-permute-start(bf16[512,256]{1,0:T(8,128)(2,1)S(1)} %add_convert_fusion.4), channel_id=1, source_target_pairs={{0,2},{2,4},{4,6},{6,8},{8,10},{10,12},{12,14},{14,0},{1,3},{3,5},... | collective-permute-start | bytes 786440 | tf_op jit(solution)/shard_map/ppermute | solution.py:282
  58.6 14.8 %collective-permute-start.8 = (bf16[512,256]{1,0:T(8,128)(2,1)S(1)}, bf16[512,256]{1,0:T(8,128)(2,1)S(1)}, u32[]{:S(2)}, u32[]{:S(2)}) collective-permute-start(bf16[512,256]{1,0:T(8,128)(2,1)S(1)} %add_convert_fusion.1), channel_id=1, source_target_pairs={{2,0},{4,2},{6,4},{8,6},{10,8},{12,10},{14,12},{0,14},{3,1},{5,3},... | collective-permute-start | bytes 786440 | tf_op jit(solution)/shard_map/ppermute | solution.py:285
  68.1 12.4 %collective-permute-start.5 = (bf16[512,256]{1,0:T(8,128)(2,1)S(1)}, bf16[512,256]{1,0:T(8,128)(2,1)S(1)}, u32[]{:S(2)}, u32[]{:S(2)}) collective-permute-start(bf16[512,256]{1,0:T(8,128)(2,1)S(1)} %add_convert_fusion.3), channel_id=1, source_target_pairs={{0,2},{2,4},{4,6},{6,8},{8,10},{10,12},{12,14},{14,0},{1,3},{3,5},... | collective-permute-start | bytes 786440 | tf_op jit(solution)/shard_map/ppermute | solution.py:282
  73.5 13.9 %collective-permute-start.9 = (bf16[512,256]{1,0:T(8,128)(2,1)S(1)}, bf16[512,256]{1,0:T(8,128)(2,1)S(1)}, u32[]{:S(2)}, u32[]{:S(2)}) collective-permute-start(bf16[512,256]{1,0:T(8,128)(2,1)S(1)} %add_convert_fusion), channel_id=1, source_target_pairs={{2,0},{4,2},{6,4},{8,6},{10,8},{12,10},{14,12},{0,14},{3,1},{5,3},... | collective-permute-start | bytes 786440 | tf_op jit(solution)/shard_map/ppermute | solution.py:285
  73.8 22.8 %collective-permute-start.20 = (bf16[32,128,128]{2,1,0:T(8,128)(2,1)S(1)}, bf16[32,128,128]{2,1,0:T(8,128)(2,1)S(1)}, u32[]{:S(2)}, u32[]{:S(2)}) collective-permute-start(bf16[32,128,128]{2,1,0:T(8,128)(2,1)S(1)} %get-tuple-element.58), channel_id=1, source_target_pairs={{0,1},{1,0},{2,3},{3,2},{4,5},{5,4},{6,7},{7,6},{8,9},{9,8},{10,11... | collective-permute-start | bytes 3145736 | tf_op jit(solution)/shard_map/ppermute | solution.py:279
  80.6 7.0 %collective-permute-start.6 = (bf16[512,256]{1,0:T(8,128)(2,1)S(1)}, bf16[512,256]{1,0:T(8,128)(2,1)S(1)}, u32[]{:S(2)}, u32[]{:S(2)}) collective-permute-start(bf16[512,256]{1,0:T(8,128)(2,1)S(1)} %add_convert_fusion.2), channel_id=1, source_target_pairs={{0,2},{2,4},{4,6},{6,8},{8,10},{10,12},{12,14},{14,0},{1,3},{3,5},... | collective-permute-start | bytes 786440 | tf_op jit(solution)/shard_map/ppermute | solution.py:282
  83.9 7.3 %collective-permute-start.16 = (bf16[256,256]{1,0:T(8,128)(2,1)S(1)}, bf16[256,256]{1,0:T(8,128)(2,1)S(1)}, u32[]{:S(2)}, u32[]{:S(2)}) collective-permute-start(bf16[256,256]{1,0:T(8,128)(2,1)S(1)} %get-tuple-element.74), channel_id=1, source_target_pairs={{2,0},{4,2},{6,4},{8,6},{10,8},{12,10},{14,12},{0,14},{3,1},{5,3},... | collective-permute-start | bytes 393224 | tf_op jit(solution)/shard_map/ppermute | solution.py:285
  87.6 16.1 %collective-permute-start.10 = (bf16[256,256]{1,0:T(8,128)(2,1)S(1)}, bf16[256,256]{1,0:T(8,128)(2,1)S(1)}, u32[]{:S(2)}, u32[]{:S(2)}) collective-permute-start(bf16[256,256]{1,0:T(8,128)(2,1)S(1)} %add_convert_fusion.19), channel_id=1, source_target_pairs={{0,1},{1,0},{2,3},{3,2},{4,5},{5,4},{6,7},{7,6},{8,9},{9,8},{10,11... | collective-permute-start | bytes 393224 | tf_op jit(solution)/shard_map/ppermute | solution.py:279
  96.5 8.1 %collective-permute-start.21 = (bf16[256,256]{1,0:T(8,128)(2,1)S(1)}, bf16[256,256]{1,0:T(8,128)(2,1)S(1)}, u32[]{:S(2)}, u32[]{:S(2)}) collective-permute-start(bf16[256,256]{1,0:T(8,128)(2,1)S(1)} %add_convert_fusion.5), channel_id=1, source_target_pairs={{0,16},{16,0},{1,17},{17,1},{2,18},{18,2},{3,19},{19,3},{4,20},{20... | collective-permute-start | bytes 393224 | tf_op jit(solution)/shard_map/ppermute | solution.py:279
  115.5 7.9 %collective-permute-start.25 = (bf16[1024,128]{1,0:T(8,128)(2,1)S(1)}, bf16[1024,128]{1,0:T(8,128)(2,1)S(1)}, u32[]{:S(2)}, u32[]{:S(2)}) collective-permute-start(bf16[1024,128]{1,0:T(8,128)(2,1)S(1)} %bitcast.28), channel_id=1, source_target_pairs={{0,2},{2,4},{4,6},{6,8},{8,10},{10,12},{12,14},{14,0},{1,3},{3,5},... | collective-permute-start | bytes 786440 | tf_op jit(solution)/shard_map/ppermute | solution.py:282
  115.6 25.3 %collective-permute-start.24 = (bf16[32,128,128]{2,1,0:T(8,128)(2,1)S(1)}, bf16[32,128,128]{2,1,0:T(8,128)(2,1)S(1)}, u32[]{:S(2)}, u32[]{:S(2)}) collective-permute-start(bf16[32,128,128]{2,1,0:T(8,128)(2,1)S(1)} %get-tuple-element.64), channel_id=1, source_target_pairs={{0,1},{1,0},{2,3},{3,2},{4,5},{5,4},{6,7},{7,6},{8,9},{9,8},{10,11... | collective-permute-start | bytes 3145736 | tf_op jit(solution)/shard_map/ppermute | solution.py:279
  123.4 6.9 %collective-permute-start.26 = (bf16[1024,128]{1,0:T(8,128)(2,1)S(1)}, bf16[1024,128]{1,0:T(8,128)(2,1)S(1)}, u32[]{:S(2)}, u32[]{:S(2)}) collective-permute-start(bf16[1024,128]{1,0:T(8,128)(2,1)S(1)} %collective-permute-done.25.refs_9_), channel_id=1, source_target_pairs={{0,2},{2,4},{4,6},{6,8},{8,10},{10,12},{12,14},{14,0},{1,3},{3,5},... | collective-permute-start | bytes 786440 | tf_op jit(solution)/shard_map/ppermute | solution.py:282
  124.6 6.7 %collective-permute-start.30 = (bf16[1024,128]{1,0:T(8,128)(2,1)S(1)}, bf16[1024,128]{1,0:T(8,128)(2,1)S(1)}, u32[]{:S(2)}, u32[]{:S(2)}) collective-permute-start(bf16[1024,128]{1,0:T(8,128)(2,1)S(1)} %collective-permute-done.29.refs_10_), channel_id=1, source_target_pairs={{2,0},{4,2},{6,4},{8,6},{10,8},{12,10},{14,12},{0,14},{3,1},{5,3},... | collective-permute-start | bytes 786440 | tf_op jit(solution)/shard_map/ppermute | solution.py:285
  131.3 9.7 %collective-permute-start.31 = (bf16[1024,128]{1,0:T(8,128)(2,1)S(1)}, bf16[1024,128]{1,0:T(8,128)(2,1)S(1)}, u32[]{:S(2)}, u32[]{:S(2)}) collective-permute-start(bf16[1024,128]{1,0:T(8,128)(2,1)S(1)} %collective-permute-done.30.refs_12_), channel_id=1, source_target_pairs={{2,0},{4,2},{6,4},{8,6},{10,8},{12,10},{14,12},{0,14},{3,1},{5,3},... | collective-permute-start | bytes 786440 | tf_op jit(solution)/shard_map/ppermute | solution.py:285
  137.1 11.5 %collective-permute-start.32 = (bf16[32,128,128]{2,1,0:T(8,128)(2,1)S(1)}, bf16[32,128,128]{2,1,0:T(8,128)(2,1)S(1)}, u32[]{:S(2)}, u32[]{:S(2)}) collective-permute-start(bf16[32,128,128]{2,1,0:T(8,128)(2,1)S(1)} %collective-permute-done.20.refs_4_), channel_id=1, source_target_pairs={{0,16},{16,0},{1,17},{17,1},{2,18},{18,2},{3,19},{19,3},{4,20},{20... | collective-permute-start | bytes 3145736 | tf_op jit(solution)/shard_map/ppermute | solution.py:279
  143.5 7.3 %collective-permute-start.33 = (bf16[32,128,128]{2,1,0:T(8,128)(2,1)S(1)}, bf16[32,128,128]{2,1,0:T(8,128)(2,1)S(1)}, u32[]{:S(2)}, u32[]{:S(2)}) collective-permute-start(bf16[32,128,128]{2,1,0:T(8,128)(2,1)S(1)} %collective-permute-done.24.refs_5_), channel_id=1, source_target_pairs={{0,16},{16,0},{1,17},{17,1},{2,18},{18,2},{3,19},{19,3},{4,20},{20... | collective-permute-start | bytes 3145736 | tf_op jit(solution)/shard_map/ppermute | solution.py:279
  158.2 37.0 %all-to-all-start.1 = ((bf16[32,256,128]{2,1,0:T(8,128)(2,1)}), bf16[32,256,128]{2,1,0:T(8,128)(2,1)S(1)}, u32[]{:S(2)}, u32[]{:S(2)}) async-start(bf16[32,256,128]{2,1,0:T(8,128)(2,1)} %bitcast.27), calls=%async_computation.1 | async-start | bytes 4194304 | tf_op jit(solution)/shard_map/all_to_all | solution.py:237
  (29 other events, 373.6 us)
